TPU v7x, 256 devices: a whole 4x4x8 slice. The times are simulated.
256 devices in a mesh: dp: 16 (over z, core), tensor: 16 (over x, y).
Axes of the slice: x: 4, y: 4, z: 8, core: 2. Of those that a mesh axis runs over, the one named last changes fastest.
Arguments:
- gate_pre: bfloat16 [16384, 14336], P('dp', 'tensor'), may hold values from -6 to 6
- up_pre: bfloat16 [16384, 14336], P('dp', 'tensor'), may hold values from -6 to 6
- grad_out: bfloat16 [16384, 4096], P(('dp', 'tensor')), may hold values from -0.59765625 to 0.59765625
- error: bfloat16 [16, 14336, 4096], P('dp', 'tensor'), may hold values from -3 to 3
- sketch: float32 [32, 4096], replicated, may hold values from -6 to 6
Outputs:
- p_factor: float32 [32, 14336], P(None, 'tensor')
- q_factor: float32 [16, 32, 4096], P('tensor')
All inputs are finite; a program needn't handle non-finite values.
Results may differ from a plain program's by a relative error of at most 0.0035.
Values may be sent and summed in bfloat16 or wider, within the bound.
A program may use at most 128 MiB of HBM per device.

v0:
```python
import jax
import jax.numpy as jnp
from jax import lax
from jax.sharding import PartitionSpec as P

HIGH = lax.Precision.HIGHEST


def contract(left_op, right_op, left_dim, right_dim):
    return lax.dot_general(
        left_op,
        right_op,
        (((left_dim,), (right_dim,)), ((), ())),
        precision=HIGH,
        preferred_element_type=jnp.float32,
    )


def gram_schmidt(rows_in):
    count = rows_in.shape[0]
    numbers = jnp.arange(count)

    def advance(column, basis):
        vector = basis[column]
        earlier = jnp.where((numbers < column)[:, None], basis, 0.0)
        for _ in range(2):
            vector = vector - jnp.dot(
                jnp.dot(earlier, vector, precision=HIGH), earlier, precision=HIGH
            )
        vector = vector / jnp.sqrt(jnp.sum(vector * vector))
        return basis.at[column].set(vector)

    return lax.fori_loop(0, count, advance, rows_in)


def shards(gate_pre, up_pre, grad_out, error, sketch):
    hidden = (jax.nn.silu(gate_pre.astype(jnp.float32)) * up_pre.astype(jnp.float32)).astype(
        jnp.bfloat16
    )
    error_dev = error[0]
    width_dev = hidden.shape[1]
    merged = lax.dot_general(
        hidden,
        lax.all_gather(grad_out, "tensor", axis=0, tiled=True),
        (((0,), (0,)), ((), ())),
        preferred_element_type=jnp.float32,
    ) + error_dev.astype(jnp.float32)
    local_left = contract(sketch, merged, 1, 1)
    summed_left = lax.psum(local_left, "dp")
    ortho = gram_schmidt(summed_left)
    local_right = contract(ortho, merged, 1, 0)
    summed_right = lax.psum(local_right, "dp")
    scale = jnp.sqrt(jnp.float32(width_dev))
    replicas = lax.axis_size("dp")
    return (ortho * scale, (summed_right / (replicas * scale))[None])


def solution(mesh):
    return jax.shard_map(
        shards,
        mesh=mesh,
        in_specs=(
            P("dp", "tensor"),
            P("dp", "tensor"),
            P(("dp", "tensor"), None),
            P("dp", "tensor", None),
            P(),
        ),
        out_specs=(P(None, "tensor"), P("tensor", None, None)),
        check_vma=False,
    )
```

profile of v0, /device:TPU:1, one launch (start us, length us, event | category | flops | bytes accessed | tf_op | source)
XLA Modules:
  0.0 690.6 jit_solution(5620164376546968291)
XLA Ops:
  8.0 82.1 %all-gather.2.cloned.1.call-done = bf16[1024,4096]{1,0:T(8,128)(2,1)} async-done(((bf16[64,4096]{1,0:T(8,128)(2,1)}), bf16[1024,4096]{1,0:T(8,128)(2,1)}) %all-gather.2.cloned.1.call-update) | async-done | bytes 8388624 | tf_op jit(solution)/shard_map/all_gather | solution.py:44
  90.0 11.8 %fusion.29 = f32[896,4096]{1,0:T(8,128)S(1)} fusion(bf16[1024,4096]{1,0:T(8,128)(2,1)} %all-gather.2.cloned.1.call-done, bf16[1024,896]{1,0:T(8,128)(2,1)} %param.10, bf16[1024,896]{1,0:T(8,128)(2,1)} %param.9), kind=kOutput, calls=%fused_computation.41 | convolution fusion | flops 7523532800 | bytes 26738688 | tf_op jit(solution)/shard_map/dot_general | solution.py:42
  101.8 5.2 copy-done.1
  107.1 16.8 %fusion.32 = f32[32,896]{1,0:T(8,128)} fusion(f32[32,4096]{1,0:T(8,128)S(1)} %copy-done, f32[896,4096]{1,0:T(8,128)S(1)} %fusion.29, bf16[1,896,4096]{2,1,0:T(8,128)(2,1)} %param.12), kind=kOutput, calls=%fused_computation.43 | convolution fusion | flops 1416626176 | bytes 22659072 | tf_op jit(solution)/shard_map/dot_general | solution.py:10
  124.1 105.9 %all-reduce.3.cloned.1.call-done = f32[32,896]{1,0:T(8,128)} async-done(((f32[32,896]{1,0:T(8,128)}), f32[32,896]{1,0:T(8,128)}) %all-reduce.3.cloned.1.call-update) | async-done | bytes 114704 | tf_op jit(solution)/shard_map/psum | solution.py:49
  230.0 329.4 %while.15 = (s32[]{:T(128)}, f32[32,896]{1,0:T(8,128)}, s32[]{:T(128)}, s32[2]{0:T(128)S(1)}, s32[1]{0:T(128)}, /*index=5*/s32[]{:T(128)}) while((s32[]{:T(128)}, f32[32,896]{1,0:T(8,128)}, s32[]{:T(128)}, s32[2]{0:T(128)S(1)}, s32[1]{0:T(128)}, /*index=5*/s32[]{:T(128)}) %tuple.55), condition=%wide.region_4.5_spmd.clone, body=%wide.region_1.4_spmd.clone.sunk | while | flops 1496362 | bytes 535319 | solution.py:33
  237.5 1.4 broadcast_select_fusion.2
  247.8 1.4 broadcast_select_fusion.2
  258.1 1.4 broadcast_select_fusion.2
  268.4 1.4 broadcast_select_fusion.2
  278.7 1.4 broadcast_select_fusion.2
  289.0 1.4 broadcast_select_fusion.2
  299.3 1.4 broadcast_select_fusion.2
  309.6 1.4 broadcast_select_fusion.2
  319.8 1.4 broadcast_select_fusion.2
  321.3 1.4 scatter.7
  330.1 1.4 broadcast_select_fusion.2
  331.6 1.4 scatter.7
  340.4 1.4 broadcast_select_fusion.2
  341.8 1.4 scatter.7
  350.7 1.4 broadcast_select_fusion.2
  352.1 1.4 scatter.7
  361.0 1.4 broadcast_select_fusion.2
  362.4 1.4 scatter.7
  371.3 1.4 broadcast_select_fusion.2
  372.7 1.4 scatter.7
  381.6 1.4 broadcast_select_fusion.2
  383.0 1.4 scatter.7
  391.9 1.4 broadcast_select_fusion.2
  393.3 1.4 scatter.7
  402.2 1.4 broadcast_select_fusion.2
  403.6 1.4 scatter.7
  412.5 1.4 broadcast_select_fusion.2
  413.9 1.4 scatter.7
  422.8 1.4 broadcast_select_fusion.2
  424.2 1.4 scatter.7
  433.1 1.4 broadcast_select_fusion.2
  434.5 1.4 scatter.7
  443.4 1.4 broadcast_select_fusion.2
  444.8 1.4 scatter.7
  453.7 1.4 broadcast_select_fusion.2
  455.1 1.4 scatter.7
  464.0 1.4 broadcast_select_fusion.2
  465.4 1.4 scatter.7
  474.3 1.4 broadcast_select_fusion.2
  475.7 1.4 scatter.7
  484.6 1.4 broadcast_select_fusion.2
  486.0 1.4 scatter.7
  494.9 1.4 broadcast_select_fusion.2
  496.3 1.4 scatter.7
  505.2 1.4 broadcast_select_fusion.2
  506.6 1.4 scatter.7
  515.5 1.4 broadcast_select_fusion.2
  516.9 1.4 scatter.7
  525.8 1.4 broadcast_select_fusion.2
  527.2 1.4 scatter.7
  536.1 1.4 broadcast_select_fusion.2
  537.5 1.4 scatter.7
  546.4 1.4 broadcast_select_fusion.2
  547.8 1.4 scatter.7
  556.7 1.4 broadcast_select_fusion.2
  559.4 14.1 %fusion.20 = f32[32,4096]{1,0:T(8,128)} fusion(f32[32,896]{1,0:T(8,128)} %get-tuple-element.88, f32[896,4096]{1,0:T(8,128)} %copy-done.1, bf16[1,896,4096]{2,1,0:T(8,128)(2,1)} %param.12), kind=kOutput, calls=%fused_computation.30 | convolution fusion | flops 1416626176 | bytes 22659072 | tf_op jit(solution)/shard_map/dot_general | solution.py:10
  574.3 107.9 %all-reduce.5.cloned.1.call-done = f32[32,4096]{1,0:T(8,128)} async-done(((f32[32,4096]{1,0:T(8,128)}), f32[32,4096]{1,0:T(8,128)}) %all-reduce.5.cloned.1.call-update) | async-done | bytes 524304 | tf_op jit(solution)/shard_map/psum | solution.py:52
  682.2 1.9 multiply_bitcast_fusion
  (375 shorter events, 231.4 us)
Async XLA Ops:
  7.2 99.9 %copy-start = (f32[32,4096]{1,0:T(8,128)S(1)}, f32[32,4096]{1,0:T(8,128)}, u32[]{:S(2)}) copy-start(f32[32,4096]{1,0:T(8,128)} %param.13) | copy-start | bytes 1572868
  7.2 82.9 %all-gather.2.cloned.1.call-start = ((), (), s32[]{:S(2)}) async-start(), calls=%async_computation | async-start | bytes 8912896 | tf_op jit(solution)/shard_map/all_gather | solution.py:44
  7.9 222.1 %all-reduce.3.cloned.1.call-start = ((), (), s32[]{:S(2)}) async-start(), calls=%async_computation.1 | async-start | bytes 229376 | tf_op jit(solution)/shard_map/psum | solution.py:49
  101.8 5.2 copy-start.1
  107.1 122.9 %copy-start.3 = (s32[2]{0:T(128)S(1)}, s32[2]{0:T(128)}, u32[]{:S(2)}) copy-start(s32[2]{0:T(128)} %constant.73.clone.2) | copy-start | bytes 28
  123.9 558.3 %all-reduce.5.cloned.1.call-start = ((), (), s32[]{:S(2)}) async-start(), calls=%async_computation.2 | async-start | bytes 1048576 | tf_op jit(solution)/shard_map/psum | solution.py:52
  559.4 14.2 %copy-start.2 = (f32[32,896]{1,0:T(8,128)S(1)}, f32[32,896]{1,0:T(8,128)}, u32[]{:S(2)}) copy-start(f32[32,896]{1,0:T(8,128)} %get-tuple-element.88) | copy-start | bytes 344068
Sparse Core Ops, SparseCore 0:
  10.4 79.5 all-gather.1
  124.0 105.9 all-reduce.2
  573.7 108.4 all-reduce.4
where the time goes:
time: 701 us; the launch traced here: 691 us
  waiting for transfers between devices  297 us (42%)
  matrix products  193 us (28%)
  other arithmetic  89.9 us (13%)
  local copies, waits for them, and re-layouts  73.8 us (11%)
  loops' own time  23.4 us (3%)
  between operations  13.8 us (2%)
    psum x1, waiting for transfers between devices, shards(): summed_right = lax.psum(local_right, 'dp')  108 us
    psum x1, waiting for transfers between devices, shards(): summed_left = lax.psum(local_left, 'dp')  106 us
    all_gather x1, waiting for transfers between devices, shards(): lax.all_gather(grad_out, 'tensor', axis=0, tiled=True)  82.1 us
    dot_general x64, matrix products, advance(): jnp.dot(jnp.dot(earlier, vector, precision=HIGH), earlier, precision=HIGH)  76.7 us
    dot_general x64, matrix products, advance(): jnp.dot(earlier, vector, precision=HIGH)  73.4 us
    another operation x64, other arithmetic  67.6 us
    scatter x32, local copies, waits for them, and re-layouts, advance(): return basis.at[column].set(vector)  43.7 us
    dot_general x2, matrix products, contract(): lax.dot_general(left_op, right_op, (((left_dim,), (right_dim,)), ((), ())...  30.9 us
  transfers between devices with their start and end apart: 3, of which 3 were waited for; matrix products, arithmetic and copies ran while one was open for 0% of the time, Pallas kernels for 0%

commit v1 on v0

v1 whole, which is shorter than its diff:
```python
import functools

import jax
import jax.numpy as jnp
from jax import lax
from jax.experimental import pallas as pl
from jax.experimental.pallas import tpu as pltpu
from jax.sharding import PartitionSpec as P

MESH = pl.DeviceIdType.MESH
HIGH = lax.Precision.HIGHEST
F32 = jnp.float32
BF16 = jnp.bfloat16
NT = (((1,), (1,)), ((), ()))
NN = (((1,), (0,)), ((), ()))

D = 4096
WIDTH = 896
TOK = 1024
R = 32
DP = 16
TENSOR = 16
X = 4
Y = 4
OWN = 64
COLS = D // Y
CH = D // DP
LC = 256


def dot(a, b, dims=NN, precision=None):
    return lax.dot_general(a, b, dims, precision=precision, preferred_element_type=F32)


def split(value):
    high = value.astype(BF16)
    low = (value - high.astype(F32)).astype(BF16)
    return jnp.concatenate([high, low], axis=0)


def fold(product):
    half = product.shape[0] // 2
    return product[:half] + product[half:]


def inverse_factor(gram):
    rows = lax.broadcasted_iota(jnp.int32, (R, 128), 0)
    lanes = lax.broadcasted_iota(jnp.int32, (R, 128), 1)
    wide = jnp.concatenate([gram, jnp.zeros((R, 128 - R), F32)], axis=1)
    wide = jnp.where(lanes == rows + R, 1.0, wide)
    for k in range(R):
        factor = wide[:, k : k + 1] / wide[k : k + 1, k : k + 1]
        wide = wide - jnp.where(rows > k, factor * wide[k : k + 1, :], 0.0)
    pivots = jnp.sum(jnp.where(lanes == rows, wide, 0.0), axis=1, keepdims=True)
    return wide * lax.rsqrt(pivots)


def kernel(
    gate_hbm, up_hbm, g_hbm, e_hbm, sk_hbm,
    p_ref, q_ref,
    gate, up, hidden, g, e, sk, sks, gcols,
    proj, proj_in, proj_all, left, left_in, left_red, left_all, leftw,
    mix, mix_in, inv, inv_in, part, part_in, right, right_in, red, qbuf,
    load_sem,
    proj_s, proj_r, gy_s, gy_r, gx_s, gx_r, ls_s, ls_r, la_s, la_r,
    mx_s, mx_r, iv_s, iv_r, pt_s, pt_r, rs_s, rs_r, ra_s, ra_r,
):
    dp = lax.axis_index("dp")
    tensor = lax.axis_index("tensor")
    mx = tensor // Y
    my = lax.rem(tensor, Y)

    loads = [
        pltpu.make_async_copy(sk_hbm, sk, load_sem.at[0]),
        pltpu.make_async_copy(g_hbm, g, load_sem.at[1]),
        pltpu.make_async_copy(gate_hbm, gate, load_sem.at[2]),
        pltpu.make_async_copy(up_hbm, up, load_sem.at[3]),
        pltpu.make_async_copy(e_hbm, e, load_sem.at[4]),
    ]
    for load in loads:
        load.start()
    own_cols = pltpu.make_async_copy(
        g_hbm.at[:, pl.ds(pl.multiple_of(my * COLS, COLS), COLS)], gcols.at[tensor], load_sem.at[5]
    )
    own_cols.start()

    barrier = pltpu.get_barrier_semaphore()

    @pl.loop(1, TENSOR)
    def _(k):
        pl.semaphore_signal(barrier, inc=1, device_id={"tensor": lax.rem(tensor + k, TENSOR)}, device_id_type=MESH)

    @pl.loop(1, DP)
    def _(k):
        pl.semaphore_signal(barrier, inc=1, device_id={"dp": lax.rem(dp + k, DP)}, device_id_type=MESH)

    def to_tensor(src, dst, send, recv, peer):
        return pltpu.make_async_remote_copy(
            src_ref=src, dst_ref=dst, send_sem=send, recv_sem=recv, device_id={"tensor": peer}, device_id_type=MESH
        )

    def to_dp(src, dst, send, recv, k):
        return pltpu.make_async_remote_copy(
            src_ref=src, dst_ref=dst, send_sem=send, recv_sem=recv,
            device_id={"dp": lax.rem(dp + k, DP)}, device_id_type=MESH,
        )

    def y_peer(k):
        return mx * Y + lax.rem(my + k, Y)

    def x_peer(k):
        return lax.rem(mx + k, X) * Y + my

    def proj_copy(k):
        return to_tensor(proj, proj_in.at[tensor], proj_s.at[k], proj_r.at[k], lax.rem(tensor + k, TENSOR))

    def gy_copy(k):
        there = lax.rem(my + k, Y)
        return to_tensor(
            g.at[:, pl.ds(pl.multiple_of(there * COLS, COLS), COLS)], gcols.at[tensor], gy_s.at[k], gy_r.at[k], y_peer(k)
        )

    def gx_copy(k):
        rows = gcols.at[pl.ds(mx * Y, Y)]
        return to_tensor(rows, rows, gx_s.at[k], gx_r.at[k], x_peer(k))

    def ls_copy(k):
        return to_dp(left.at[lax.rem(dp + k, DP)], left_in.at[k], ls_s.at[k], ls_r.at[k], k)

    def la_copy(k):
        return to_dp(left_red, left_all.at[dp], la_s.at[k], la_r.at[k], k)

    def mix_copy(k):
        return to_tensor(mix, mix_in.at[k], mx_s.at[k], mx_r.at[k], y_peer(k))

    def inv_copy(k):
        return to_tensor(inv, inv_in.at[k], iv_s.at[k], iv_r.at[k], y_peer(k))

    def part_copy(k):
        return to_tensor(part.at[k], part_in.at[k], pt_s.at[k], pt_r.at[k], y_peer(k))

    def rs_copy(k):
        return to_dp(right.at[lax.rem(dp + k, DP)], right_in.at[k], rs_s.at[k], rs_r.at[k], k)

    def ra_copy(k):
        return to_dp(red, qbuf.at[dp], ra_s.at[k], ra_r.at[k], k)

    def start(copy, count):
        pl.loop(1, count)(lambda k: copy(k).start())

    def arrived(copy, count):
        pl.loop(1, count)(lambda k: copy(k).wait_recv())

    def sent(copy, count):
        pl.loop(1, count)(lambda k: copy(k).wait_send())

    loads[0].wait()
    sks[...] = split(sk[...])
    loads[1].wait()
    projected = fold(dot(sks[...], g[...], NT))
    high = projected.astype(BF16)
    low = (projected - high.astype(F32)).astype(BF16)
    proj[...] = jnp.concatenate([high, low], axis=1)
    proj_in[tensor] = proj[...]

    pl.semaphore_wait(barrier, TENSOR - 1 + DP - 1)
    start(proj_copy, TENSOR)
    start(gy_copy, Y)

    loads[2].wait()
    loads[3].wait()

    @pl.loop(0, TOK // 64)
    def _(j):
        rows = pl.ds(pl.multiple_of(j * 64, 64), 64)
        v = gate[rows, :].astype(F32)
        u = up[rows, :].astype(F32)
        hidden[rows, :] = (v / (1.0 + jnp.exp(-v)) * u).astype(BF16)

    arrived(gy_copy, Y)
    own_cols.wait()
    start(gx_copy, X)

    loads[4].wait()
    for j in range(WIDTH // 128):
        leftw[:, j * 128 : (j + 1) * 128] = fold(dot(sks[...], e[j * 128 : (j + 1) * 128, :], NT))

    arrived(proj_copy, TENSOR)
    for j in range(TENSOR // 2):
        a = proj_in[2 * j]
        b = proj_in[2 * j + 1]
        proj_all[0:R, j * 128 : (j + 1) * 128] = jnp.concatenate([a[:, :OWN], b[:, :OWN]], axis=1)
        proj_all[R : 2 * R, j * 128 : (j + 1) * 128] = jnp.concatenate([a[:, OWN:], b[:, OWN:]], axis=1)
    mine = leftw[...] + fold(dot(proj_all[...], hidden[...]))
    mine = jnp.concatenate([mine, jnp.zeros((R, Y * LC - WIDTH), F32)], axis=1)
    for p in range(DP):
        left[p] = mine[8 * (p // 4) : 8 * (p // 4) + 8, LC * (p % 4) : LC * (p % 4) + LC]

    start(ls_copy, DP)
    arrived(ls_copy, DP)
    left_red[...] = left[dp] + functools.reduce(jnp.add, [left_in[k] for k in range(1, DP)])
    left_all[dp] = left_red[...]
    start(la_copy, DP)
    arrived(la_copy, DP)
    for p in range(DP):
        width = min(LC, WIDTH - LC * (p % 4))
        leftw[8 * (p // 4) : 8 * (p // 4) + 8, LC * (p % 4) : LC * (p % 4) + width] = left_all[p][:, :width]

    whole = leftw[...]
    mix[...] = split(fold(dot(split(whole), hidden[...], NT)))
    start(mix_copy, Y)

    factor = inverse_factor(dot(whole, whole, NT, HIGH))
    inv[...] = factor
    start(inv_copy, Y)
    ortho = dot(factor[:, R : 2 * R], whole, NN, HIGH)
    p_ref[...] = ortho * (float(WIDTH) ** 0.5)
    ortho2 = split(ortho)

    @pl.loop(0, DP)
    def _(j):
        right[j] = fold(dot(ortho2, e[:, pl.ds(pl.multiple_of(j * CH, CH), CH)]))

    arrived(gx_copy, X)
    columns = gcols.reshape(TOK, COLS)

    def product(mixed, factor_there, target):
        value = mixed[0:R].astype(F32) + mixed[R : 2 * R].astype(F32)
        value = split(dot(factor_there[:, R : 2 * R], value, NN, HIGH))
        for j in range(Y):
            target(j, fold(dot(value, columns[:, j * CH : (j + 1) * CH])))

    def send_part(k):
        mix_copy(k).wait_recv()
        inv_copy(k).wait_recv()

        def keep(j, block):
            part[lax.rem(Y - k, Y), j] = block

        product(mix_in[k], inv_in[k], keep)
        part_copy(lax.rem(Y - k, Y)).start()

    pl.loop(1, Y)(send_part)

    def add_own(j, block):
        right[my * Y + j] += block

    product(mix[...], factor, add_own)

    @pl.loop(1, Y)
    def _(k):
        part_copy(k).wait_recv()
        there = lax.rem(my + Y - k, Y)
        for j in range(Y):
            right[there * Y + j] += part_in[k, j]

    start(rs_copy, DP)
    arrived(rs_copy, DP)
    total = right[dp] + functools.reduce(jnp.add, [right_in[k] for k in range(1, DP)])
    red[...] = (total * (1.0 / (DP * float(WIDTH) ** 0.5))).astype(BF16)
    qbuf[dp] = red[...]
    start(ra_copy, DP)
    arrived(ra_copy, DP)
    for p in range(DP):
        q_ref[:, p * CH : (p + 1) * CH] = qbuf[p]

    sent(proj_copy, TENSOR)
    sent(gy_copy, Y)
    sent(gx_copy, X)
    sent(ls_copy, DP)
    sent(la_copy, DP)
    sent(mix_copy, Y)
    sent(inv_copy, Y)
    sent(part_copy, Y)
    sent(rs_copy, DP)
    sent(ra_copy, DP)


def shards(gate_pre, up_pre, grad_out, error, sketch):
    vmem = pltpu.VMEM
    dma = pltpu.SemaphoreType.DMA
    scratch = [
        vmem((TOK, WIDTH), BF16),
        vmem((TOK, WIDTH), BF16),
        vmem((TOK, WIDTH), BF16),
        vmem((OWN, D), BF16),
        vmem((WIDTH, D), BF16),
        vmem((R, D), F32),
        vmem((2 * R, D), BF16),
        vmem((TENSOR, OWN, COLS), BF16),
        vmem((R, 2 * OWN), BF16),
        vmem((TENSOR, R, 2 * OWN), BF16),
        vmem((2 * R, TOK), BF16),
        vmem((DP, 8, LC), F32),
        vmem((DP, 8, LC), F32),
        vmem((8, LC), F32),
        vmem((DP, 8, LC), F32),
        vmem((R, WIDTH), F32),
        vmem((2 * R, TOK), BF16),
        vmem((Y, 2 * R, TOK), BF16),
        vmem((R, 128), F32),
        vmem((Y, R, 128), F32),
        vmem((Y, Y, R, CH), F32),
        vmem((Y, Y, R, CH), F32),
        vmem((DP, R, CH), F32),
        vmem((DP, R, CH), F32),
        vmem((R, CH), BF16),
        vmem((DP, R, CH), BF16),
        dma((6,)),
        dma((TENSOR,)), dma((TENSOR,)),
        dma((Y,)), dma((Y,)),
        dma((X,)), dma((X,)),
        dma((DP,)), dma((DP,)),
        dma((DP,)), dma((DP,)),
        dma((Y,)), dma((Y,)),
        dma((Y,)), dma((Y,)),
        dma((Y,)), dma((Y,)),
        dma((DP,)), dma((DP,)),
        dma((DP,)), dma((DP,)),
    ]
    p_factor, q_factor = pl.pallas_call(
        kernel,
        out_shape=(jax.ShapeDtypeStruct((R, WIDTH), F32), jax.ShapeDtypeStruct((R, D), BF16)),
        in_specs=[pl.BlockSpec(memory_space=pl.ANY)] * 5,
        out_specs=(pl.BlockSpec(memory_space=pltpu.VMEM), pl.BlockSpec(memory_space=pltpu.VMEM)),
        scratch_shapes=scratch,
        compiler_params=pltpu.CompilerParams(
            collective_id=0, has_side_effects=True, vmem_limit_bytes=56 * 1024 * 1024
        ),
    )(gate_pre, up_pre, grad_out, error[0], sketch)
    return p_factor, q_factor.astype(F32)[None]


def solution(mesh):
    return jax.shard_map(
        shards,
        mesh=mesh,
        in_specs=(
            P("dp", "tensor"),
            P("dp", "tensor"),
            P(("dp", "tensor"), None),
            P("dp", "tensor", None),
            P(),
        ),
        out_specs=(P(None, "tensor"), P("tensor", None, None)),
        check_vma=False,
    )
```

time: 701 us -> 83.5 us (0.12); the launches traced: 691 us -> 82 us
  waiting for transfers between devices: 297 us -> 0 us
  matrix products: 193 us -> 0 us
  other arithmetic: 89.9 us -> 1.78 us
  Pallas kernels: 0 us -> 78 us
  local copies, waits for them, and re-layouts: 73.8 us -> 1.55 us
  loops' own time: 23.4 us -> 0 us
  between operations: 13.8 us -> 0.64 us
    psum x2 -> x0, waiting for transfers between devices: 214 us -> none  [the longest x1 108 us: shards(): summed_right = lax.psum(local_right, 'dp')]
    dot_general x131 -> x0, matrix products: 193 us -> none  [the longest x64 76.7 us: advance(): jnp.dot(jnp.dot(earlier, vector, precision=HIGH), earlier, precision=HIGH)]
    all_gather x1 -> x0, waiting for transfers between devices: 82.1 us -> none  [shards(): lax.all_gather(grad_out, 'tensor', axis=0, tiled=True)]
    pallas_call x0 -> x1, Pallas kernels: none -> 78 us  [shards(): pl.pallas_call(kernel, out_shape=(jax.ShapeDtypeStruct((R, WIDTH), F32),...]
    another operation x64 -> x0, other arithmetic: 67.6 us -> none
    scatter x32 -> x0, local copies, waits for them, and re-layouts: 43.7 us -> none  [advance(): return basis.at[column].set(vector)]
    dynamic_slice x32 -> x0, local copies, waits for them, and re-layouts: 24.7 us -> none  [advance(): vector = basis[column]]
    another operation x1 -> x0, loops' own time: 23.4 us -> none  [gram_schmidt(): return lax.fori_loop(0, count, advance, rows_in)]
  transfers between devices with their start and end apart: 3 -> 0, of which waited for: 3 -> 0; matrix products, arithmetic and copies ran while one was open for 0% -> 0% of each run, Pallas kernels for 0% -> 0%
where the time goes in v1:
time: 83.5 us; the launch traced here: 82 us
  Pallas kernels  78 us (93%)
  other arithmetic  1.78 us (2%)
  local copies, waits for them, and re-layouts  1.55 us (2%)
    pallas_call x1, Pallas kernels, shards(): pl.pallas_call(kernel, out_shape=(jax.ShapeDtypeStruct((R, WIDTH), F32),...  78 us
    broadcast_in_dim x1, other arithmetic, shards(): return (p_factor, q_factor.astype(F32)[None])  1.78 us

profile of v1, /device:TPU:1, one launch (start us, length us, event | category | flops | bytes accessed | tf_op | source)
XLA Modules:
  0.0 82.0 jit_solution(13572597160650840077)
XLA Ops:
  0.6 78.0 %shard_map.68 = (f32[32,896]{1,0:T(8,128)}, bf16[32,4096]{1,0:T(8,128)(2,1)}) custom-call(bf16[1024,896]{1,0:T(8,128)(2,1)} %gate_hbm.1, bf16[1024,896]{1,0:T(8,128)(2,1)} %up_hbm.1, bf16[64,4096]{1,0:T(8,128)(2,1)} %g_hbm.1, bf16[896,4096]{1,0:T(8,128)(2,1)} %bitcast.4, f32[32,4096]{1,0:T(8,128)} %sk_hbm.1), custom_call_target="tpu_custom_call" | custom-call | tf_op jit(solution)/shard_map/pallas_call | solution.py:321
  78.6 1.8 %bitcast_convert_fusion = f32[1,32,4096]{2,1,0:T(8,128)} fusion(bf16[32,4096]{1,0:T(8,128)(2,1)} %get-tuple-element.5), kind=kLoop, calls=%fused_computation | loop fusion | flops 131072 | bytes 786432 | tf_op jit(solution)/shard_map/broadcast_in_dim | solution.py:331
  80.4 1.6 %copy.8 = f32[32,896]{1,0:T(8,128)} copy(f32[32,896]{1,0:T(8,128)} %get-tuple-element.8) | data formatting | bytes 229376

commit v2 on v1

v2 whole, which is shorter than its diff:
```python
import functools

import jax
import jax.numpy as jnp
from jax import lax
from jax.experimental import pallas as pl
from jax.experimental.pallas import tpu as pltpu
from jax.sharding import PartitionSpec as P

MESH = pl.DeviceIdType.MESH
HIGH = lax.Precision.HIGHEST
F32 = jnp.float32
BF16 = jnp.bfloat16
NT = (((1,), (1,)), ((), ()))
NN = (((1,), (0,)), ((), ()))

D = 4096
WIDTH = 896
TOK = 1024
R = 32
DP = 16
TENSOR = 16
X = 4
Y = 4
Z = 8
OWN = 64
HALF = D // 2
COLS = HALF // 4
CH = D // DP
LC = 256


def dot(a, b, dims=NN, precision=None):
    return lax.dot_general(a, b, dims, precision=precision, preferred_element_type=F32)


def split(value):
    high = value.astype(BF16)
    low = (value - high.astype(F32)).astype(BF16)
    return jnp.concatenate([high, low], axis=0)


def fold(product):
    half = product.shape[0] // 2
    return product[:half] + product[half:]


def inverse_factor(gram):
    rows = lax.broadcasted_iota(jnp.int32, (R, 128), 0)
    lanes = lax.broadcasted_iota(jnp.int32, (R, 128), 1)
    wide = jnp.concatenate([gram, jnp.zeros((R, 128 - R), F32)], axis=1)
    wide = jnp.where(lanes == rows + R, 1.0, wide)
    for k in range(R):
        factor = wide[:, k : k + 1] / wide[k : k + 1, k : k + 1]
        wide = wide - jnp.where(rows > k, factor * wide[k : k + 1, :], 0.0)
    pivots = jnp.sum(jnp.where(lanes == rows, wide, 0.0), axis=1, keepdims=True)
    return (wide * lax.rsqrt(pivots))[:, R : 2 * R]


def kernel(
    gate_hbm, up_hbm, g_hbm, e_hbm, sk_hbm,
    p_ref, q_ref,
    gate, up, hidden, g, e, sk, sks, gcols,
    proj, proj_in, proj_all, left, left_in, left_red, left_all, leftw,
    mix, errors, errors_in, part, part_in, psum, swap_in, right, right_in, red, qbuf,
    load_sem,
    proj_s, proj_r, gs_s, gs_r, gl_s, gl_r, ls_s, ls_r, la_s, la_r,
    mx_s, mx_r, ec_s, ec_r, pc_s, pc_r, sw_s, sw_r, rs_s, rs_r, ra_s, ra_r, fw_s, fw_r,
):
    dp = lax.axis_index("dp")
    tensor = lax.axis_index("tensor")
    mx = tensor // Y
    my = lax.rem(tensor, Y)
    mz = dp // 2
    core = lax.rem(dp, 2)

    barrier = pltpu.get_barrier_semaphore()

    @pl.loop(1, TENSOR)
    def _(k):
        pl.semaphore_signal(barrier, inc=1, device_id={"tensor": lax.rem(tensor + k, TENSOR)}, device_id_type=MESH)

    @pl.loop(1, DP)
    def _(k):
        pl.semaphore_signal(barrier, inc=1, device_id={"dp": lax.rem(dp + k, DP)}, device_id_type=MESH)

    def cols(half, place):
        return pl.ds(pl.multiple_of(half * HALF + place * COLS, COLS), COLS)

    loads = [
        pltpu.make_async_copy(sk_hbm, sk, load_sem.at[0]),
        pltpu.make_async_copy(g_hbm, g, load_sem.at[1]),
        pltpu.make_async_copy(gate_hbm, gate, load_sem.at[2]),
        pltpu.make_async_copy(up_hbm, up, load_sem.at[3]),
        pltpu.make_async_copy(e_hbm, e, load_sem.at[4]),
        pltpu.make_async_copy(g_hbm.at[:, cols(0, my)], gcols.at[0, tensor], load_sem.at[5]),
        pltpu.make_async_copy(g_hbm.at[:, cols(1, mx)], gcols.at[1, tensor], load_sem.at[6]),
    ]
    for load in loads:
        load.start()

    def remote(src, dst, send, recv, peer):
        return pltpu.make_async_remote_copy(
            src_ref=src, dst_ref=dst, send_sem=send, recv_sem=recv, device_id=peer, device_id_type=MESH
        )

    def y_peer(k):
        return {"tensor": mx * Y + lax.rem(my + k, Y)}

    def x_peer(k):
        return {"tensor": lax.rem(mx + k, X) * Y + my}

    def dp_peer(k):
        return {"dp": lax.rem(dp + k, DP)}

    def z_peer(k):
        return {"dp": lax.rem(mz + k, Z) * 2 + core}

    other_core = {"dp": mz * 2 + 1 - core}

    def proj_copy(k):
        return remote(
            proj, proj_in.at[tensor], proj_s.at[k], proj_r.at[k], {"tensor": lax.rem(tensor + k, TENSOR)}
        )

    def ga_copy(k):
        return remote(
            g.at[:, cols(0, lax.rem(my + k, Y))], gcols.at[0, tensor], gs_s.at[0, k], gs_r.at[0, k], y_peer(k)
        )

    def gb_copy(k):
        return remote(
            g.at[:, cols(1, lax.rem(mx + k, X))], gcols.at[1, tensor], gs_s.at[1, k], gs_r.at[1, k], x_peer(k)
        )

    def gax_copy(k):
        rows = gcols.at[0, pl.ds(mx * Y, Y)]
        return remote(rows, rows, gl_s.at[0, k], gl_r.at[0, k], x_peer(k))

    def gby_copy(i, k):
        row = gcols.at[1, i * Y + my]
        return remote(row, row, gl_s.at[1 + i, k], gl_r.at[1 + i, k], y_peer(k))

    def ls_copy(k):
        return remote(left.at[lax.rem(dp + k, DP)], left_in.at[k], ls_s.at[k], ls_r.at[k], dp_peer(k))

    def la_copy(k):
        return remote(left_red, left_all.at[dp], la_s.at[k], la_r.at[k], dp_peer(k))

    def mixa_copy(k):
        return remote(mix.at[0, 0], mix.at[0, k], mx_s.at[0, k], mx_r.at[0, k], y_peer(k))

    def mixb_copy(k):
        return remote(mix.at[0, 0], mix.at[1, k], mx_s.at[1, k], mx_r.at[1, k], x_peer(k))

    errors_copy = remote(errors.at[1 - core], errors_in, ec_s.at[0], ec_r.at[0], other_core)

    def part_copy(half):
        return remote(part.at[1 - core, half], part_in.at[half], pc_s.at[half], pc_r.at[half], other_core)

    def swapa_copy(k):
        return remote(psum.at[0, k], swap_in.at[0, k], sw_s.at[0, k], sw_r.at[0, k], y_peer(k))

    def swapb_copy(k):
        return remote(psum.at[1, k], swap_in.at[1, k], sw_s.at[1, k], sw_r.at[1, k], x_peer(k))

    def rs_copy(k):
        return remote(right.at[lax.rem(mz + k, Z)], right_in.at[k], rs_s.at[k], rs_r.at[k], z_peer(k))

    def ra_copy(k):
        return remote(red, qbuf.at[dp], ra_s.at[k], ra_r.at[k], z_peer(k))

    def fw_copy(k):
        chunk = qbuf.at[lax.rem(mz + Z - k, Z) * 2 + core]
        return remote(chunk, chunk, fw_s.at[k], fw_r.at[k], other_core)

    def start(copy, count):
        pl.loop(1, count)(lambda k: copy(k).start())

    def arrived(copy, count):
        pl.loop(1, count)(lambda k: copy(k).wait_recv())

    def sent(copy, count):
        pl.loop(1, count)(lambda k: copy(k).wait_send())

    loads[0].wait()
    sks[...] = split(sk[...])
    loads[1].wait()
    projected = fold(dot(sks[...], g[...], NT))
    high = projected.astype(BF16)
    low = (projected - high.astype(F32)).astype(BF16)
    proj[...] = jnp.concatenate([high, low], axis=1)
    proj_in[tensor] = proj[...]

    pl.semaphore_wait(barrier, TENSOR - 1 + DP - 1)
    start(proj_copy, TENSOR)
    start(ga_copy, Y)
    start(gb_copy, X)

    loads[2].wait()
    loads[3].wait()

    @pl.loop(0, TOK // 64)
    def _(j):
        rows = pl.ds(pl.multiple_of(j * 64, 64), 64)
        v = gate[rows, :].astype(F32)
        u = up[rows, :].astype(F32)
        hidden[rows, :] = (v / (1.0 + jnp.exp(-v)) * u).astype(BF16)

    loads[4].wait()
    for at in range(0, WIDTH, 256):
        to = min(at + 256, WIDTH)
        leftw[:, at:to] = fold(dot(sks[...], e[at:to, :], NT))

    arrived(proj_copy, TENSOR)
    for j in range(TENSOR // 2):
        a = proj_in[2 * j]
        b = proj_in[2 * j + 1]
        proj_all[0:R, j * 128 : (j + 1) * 128] = jnp.concatenate([a[:, :OWN], b[:, :OWN]], axis=1)
        proj_all[R : 2 * R, j * 128 : (j + 1) * 128] = jnp.concatenate([a[:, OWN:], b[:, OWN:]], axis=1)
    mine = leftw[...] + fold(dot(proj_all[...], hidden[...]))
    mine = jnp.concatenate([mine, jnp.zeros((R, 4 * LC - WIDTH), F32)], axis=1)
    for p in range(DP):
        left[p] = mine[8 * (p // 4) : 8 * (p // 4) + 8, LC * (p % 4) : LC * (p % 4) + LC]

    start(ls_copy, DP)
    loads[5].wait()
    loads[6].wait()
    arrived(ga_copy, Y)
    start(gax_copy, X)
    arrived(gb_copy, X)

    @pl.loop(0, X)
    def _(i):
        start(functools.partial(gby_copy, i), Y)

    arrived(ls_copy, DP)
    left_red[...] = left[dp] + functools.reduce(jnp.add, [left_in[k] for k in range(1, DP)])
    left_all[dp] = left_red[...]
    start(la_copy, DP)
    arrived(la_copy, DP)
    for p in range(DP):
        width = min(LC, WIDTH - LC * (p % 4))
        leftw[8 * (p // 4) : 8 * (p // 4) + 8, LC * (p % 4) : LC * (p % 4) + width] = left_all[p][:, :width]

    whole = split(leftw[...])
    mixed = split(fold(dot(whole, hidden[...], NT)))
    mix[0, 0] = mixed
    start(mixa_copy, Y)
    start(mixb_copy, X)
    mix[1, 0] = mixed

    @pl.loop(0, Z)
    def _(j):
        for half in range(2):
            at = pl.multiple_of(j * 2 * CH + half * CH, CH)
            errors[half, j] = fold(dot(whole, e[:, pl.ds(at, CH)]))

    errors_copy.start()

    arrived(gax_copy, X)

    def product(side):
        rows = mix[side].reshape(4 * 2 * R, TOK)
        for half in range(2):
            block = dot(rows, gcols[side, :, :, half * CH : (half + 1) * CH].reshape(TOK, CH))
            for k in range(4):
                part[half, side, (4 - k) % 4] = fold(block[2 * R * k : 2 * R * (k + 1)])

    arrived(mixa_copy, Y)
    product(0)
    part_copy(0).start()

    @pl.loop(0, X)
    def _(i):
        arrived(functools.partial(gby_copy, i), Y)

    arrived(mixb_copy, X)
    product(1)
    part_copy(1).start()

    errors_copy.wait_recv()
    for j in range(Z):
        right[j] = errors[core, j] + errors_in[j]
    for side, copy in ((0, swapa_copy), (1, swapb_copy)):
        part_copy(side).wait_recv()
        for k in range(4):
            psum[side, k] = part[core, side, k] + part_in[side, k]
        start(copy, 4)
    right[my] += psum[0, 0]
    right[4 + mx] += psum[1, 0]

    @pl.loop(1, 4)
    def _(k):
        swapa_copy(k).wait_recv()
        right[lax.rem(my + 4 - k, 4)] += swap_in[0, k]

    @pl.loop(1, 4)
    def _(k):
        swapb_copy(k).wait_recv()
        right[4 + lax.rem(mx + 4 - k, 4)] += swap_in[1, k]

    start(rs_copy, Z)

    full = leftw[...]
    factor = inverse_factor(dot(full, full, NT, HIGH))
    p_ref[...] = dot(factor, full, NN, HIGH) * (float(WIDTH) ** 0.5)
    sent(proj_copy, TENSOR)
    sent(ga_copy, Y)
    sent(gb_copy, X)
    sent(gax_copy, X)

    @pl.loop(0, X)
    def _(i):
        sent(functools.partial(gby_copy, i), Y)

    sent(ls_copy, DP)
    sent(la_copy, DP)
    sent(mixa_copy, Y)
    sent(mixb_copy, X)
    errors_copy.wait_send()
    part_copy(0).wait_send()
    part_copy(1).wait_send()
    sent(swapa_copy, Y)
    sent(swapb_copy, X)

    arrived(rs_copy, Z)
    total = right[mz] + functools.reduce(jnp.add, [right_in[k] for k in range(1, Z)])
    total = dot(factor, total, NN, HIGH) * (1.0 / (DP * float(WIDTH) ** 0.5))
    red[...] = total.astype(BF16)
    start(ra_copy, Z)
    qbuf[dp] = red[...]
    fw_copy(0).start()

    @pl.loop(1, Z)
    def _(k):
        ra_copy(k).wait_recv()
        fw_copy(k).start()

    pl.loop(0, Z)(lambda k: fw_copy(k).wait_recv())
    for p in range(DP):
        q_ref[:, p * CH : (p + 1) * CH] = qbuf[p]

    sent(rs_copy, Z)
    sent(ra_copy, Z)
    pl.loop(0, Z)(lambda k: fw_copy(k).wait_send())


def finish(p_in, q_in, p_out, q_out):
    p_out[...] = p_in[...]
    q_out[0] = q_in[...].astype(F32)


def shards(gate_pre, up_pre, grad_out, error, sketch):
    vmem = pltpu.VMEM
    dma = pltpu.SemaphoreType.DMA
    scratch = [
        vmem((TOK, WIDTH), BF16),
        vmem((TOK, WIDTH), BF16),
        vmem((TOK, WIDTH), BF16),
        vmem((OWN, D), BF16),
        vmem((WIDTH, D), BF16),
        vmem((R, D), F32),
        vmem((2 * R, D), BF16),
        vmem((2, TENSOR, OWN, COLS), BF16),
        vmem((R, 2 * OWN), BF16),
        vmem((TENSOR, R, 2 * OWN), BF16),
        vmem((2 * R, TOK), BF16),
        vmem((DP, 8, LC), F32),
        vmem((DP, 8, LC), F32),
        vmem((8, LC), F32),
        vmem((DP, 8, LC), F32),
        vmem((R, WIDTH), F32),
        vmem((2, 4, 2 * R, TOK), BF16),
        vmem((2, Z, R, CH), F32),
        vmem((Z, R, CH), F32),
        vmem((2, 2, 4, R, CH), F32),
        vmem((2, 4, R, CH), F32),
        vmem((2, 4, R, CH), F32),
        vmem((2, 4, R, CH), F32),
        vmem((Z, R, CH), F32),
        vmem((Z, R, CH), F32),
        vmem((R, CH), BF16),
        vmem((DP, R, CH), BF16),
        dma((7,)),
        dma((TENSOR,)), dma((TENSOR,)),
        dma((2, 4)), dma((2, 4)),
        dma((5, 4)), dma((5, 4)),
        dma((DP,)), dma((DP,)),
        dma((DP,)), dma((DP,)),
        dma((2, 4)), dma((2, 4)),
        dma((1,)), dma((1,)),
        dma((2,)), dma((2,)),
        dma((2, 4)), dma((2, 4)),
        dma((Z,)), dma((Z,)),
        dma((Z,)), dma((Z,)),
        dma((Z,)), dma((Z,)),
    ]
    p_factor, q_factor = pl.pallas_call(
        kernel,
        out_shape=(jax.ShapeDtypeStruct((R, WIDTH), F32), jax.ShapeDtypeStruct((R, D), BF16)),
        in_specs=[pl.BlockSpec(memory_space=pl.ANY)] * 5,
        out_specs=(pl.BlockSpec(memory_space=pltpu.VMEM), pl.BlockSpec(memory_space=pltpu.VMEM)),
        scratch_shapes=scratch,
        compiler_params=pltpu.CompilerParams(
            collective_id=0, has_side_effects=True, vmem_limit_bytes=56 * 1024 * 1024
        ),
    )(gate_pre, up_pre, grad_out, error[0], sketch)
    return pl.pallas_call(
        finish,
        out_shape=(jax.ShapeDtypeStruct((R, WIDTH), F32), jax.ShapeDtypeStruct((1, R, D), F32)),
    )(p_factor, q_factor)


def solution(mesh):
    return jax.shard_map(
        shards,
        mesh=mesh,
        in_specs=(
            P("dp", "tensor"),
            P("dp", "tensor"),
            P(("dp", "tensor"), None),
            P("dp", "tensor", None),
            P(),
        ),
        out_specs=(P(None, "tensor"), P("tensor", None, None)),
        check_vma=False,
    )
```

time: 83.5 us -> 65.1 us (0.78); the launches traced: 82 us -> 65 us
  Pallas kernels: 78 us -> 64.4 us
  other arithmetic: 1.78 us -> 0 us
  local copies, waits for them, and re-layouts: 1.55 us -> 0 us
    pallas_call x1, Pallas kernels: 78 us -> 62.5 us  [shards(): pl.pallas_call(kernel, out_shape=(jax.ShapeDtypeStruct((R, WIDTH), F32),...]
    pallas_call x0 -> x1, Pallas kernels: none -> 1.85 us  [shards(): pl.pallas_call(finish, out_shape=(jax.ShapeDtypeStruct((R, WIDTH), F32),...]
    broadcast_in_dim x1 -> x0, other arithmetic: 1.78 us -> none  [shards(): return (p_factor, q_factor.astype(F32)[None])]
    unnamed x1 -> x0, local copies, waits for them, and re-layouts: 1.55 us -> none
where the time goes in v2:
time: 65.1 us; the launch traced here: 65 us
  Pallas kernels  64.4 us (99%)
    pallas_call x1, Pallas kernels, shards(): pl.pallas_call(kernel, out_shape=(jax.ShapeDtypeStruct((R, WIDTH), F32),...  62.5 us
    pallas_call x1, Pallas kernels, shards(): pl.pallas_call(finish, out_shape=(jax.ShapeDtypeStruct((R, WIDTH), F32),...  1.85 us

profile of v2, /device:TPU:1, one launch (start us, length us, event | category | flops | bytes accessed | tf_op | source)
XLA Modules:
  0.0 65.0 jit_solution(6467186611709253290)
XLA Ops:
  0.6 62.5 %shard_map.68 = (f32[32,896]{1,0:T(8,128)}, bf16[32,4096]{1,0:T(8,128)(2,1)}) custom-call(bf16[1024,896]{1,0:T(8,128)(2,1)} %gate_hbm.1, bf16[1024,896]{1,0:T(8,128)(2,1)} %up_hbm.1, bf16[64,4096]{1,0:T(8,128)(2,1)} %g_hbm.1, bf16[896,4096]{1,0:T(8,128)(2,1)} %bitcast.1, f32[32,4096]{1,0:T(8,128)} %sk_hbm.1), custom_call_target="tpu_custom_call" | custom-call | tf_op jit(solution)/shard_map/pallas_call | solution.py:399
  63.2 1.9 %shard_map.69 = (f32[32,896]{1,0:T(8,128)}, f32[1,32,4096]{2,1,0:T(8,128)}) custom-call(f32[32,896]{1,0:T(8,128)} %get-tuple-element.4.p_in, bf16[32,4096]{1,0:T(8,128)(2,1)} %get-tuple-element.5.q_in), custom_call_target="tpu_custom_call" | custom-call | tf_op jit(solution)/shard_map/pallas_call | solution.py:409

commit v3 on v2

v3 whole, which is shorter than its diff:
```python
import functools

import jax
import jax.numpy as jnp
from jax import lax
from jax.experimental import pallas as pl
from jax.experimental.pallas import tpu as pltpu
from jax.sharding import PartitionSpec as P

MESH = pl.DeviceIdType.MESH
HIGH = lax.Precision.HIGHEST
F32 = jnp.float32
BF16 = jnp.bfloat16
NT = (((1,), (1,)), ((), ()))
NN = (((1,), (0,)), ((), ()))

D = 4096
WIDTH = 896
TOK = 1024
R = 32
DP = 16
TENSOR = 16
X = 4
Y = 4
Z = 8
OWN = 64
HALF = D // 2
COLS = HALF // 4
CH = D // DP
LC = 256


def dot(a, b, dims=NN, precision=None):
    return lax.dot_general(a, b, dims, precision=precision, preferred_element_type=F32)


def split(value):
    high = value.astype(BF16)
    low = (value - high.astype(F32)).astype(BF16)
    return jnp.concatenate([high, low], axis=0)


def fold(product):
    half = product.shape[0] // 2
    return product[:half] + product[half:]


def inverse_factor(gram):
    rows = lax.broadcasted_iota(jnp.int32, (R, 128), 0)
    lanes = lax.broadcasted_iota(jnp.int32, (R, 128), 1)
    wide = jnp.concatenate([gram, jnp.zeros((R, 128 - R), F32)], axis=1)
    wide = jnp.where(lanes == rows + R, 1.0, wide)
    for k in range(R):
        factor = wide[:, k : k + 1] / wide[k : k + 1, k : k + 1]
        wide = wide - jnp.where(rows > k, factor * wide[k : k + 1, :], 0.0)
    pivots = jnp.sum(jnp.where(lanes == rows, wide, 0.0), axis=1, keepdims=True)
    return (wide * lax.rsqrt(pivots))[:, R : 2 * R]


def kernel(
    gate_hbm, up_hbm, g_hbm, e_hbm, sk_hbm,
    p_ref, q_ref,
    gate, up, hidden, g, e, sk, sks, gcols,
    proj, proj_in, proj_all, left, left_half, left_in, left_red, left_all, leftw,
    mix, errors, errors_in, esum, esum_in, part, part_in, psum, psum_in, red, qbuf,
    load_sem,
    proj_s, proj_r, gs_s, gs_r, gl_s, gl_r, lc_s, lc_r, ls_s, ls_r, la_s, la_r, lf_s, lf_r,
    mx_s, mx_r, ec_s, ec_r, es_s, es_r, pc_s, pc_r, ps_s, ps_r, ra_s, ra_r, fw_s, fw_r,
):
    dp = lax.axis_index("dp")
    tensor = lax.axis_index("tensor")
    mx = tensor // Y
    my = lax.rem(tensor, Y)
    mz = dp // 2
    core = lax.rem(dp, 2)

    def cols(half, place):
        return pl.ds(pl.multiple_of(half * HALF + place * COLS, COLS), COLS)

    loads = [
        pltpu.make_async_copy(sk_hbm, sk, load_sem.at[0]),
        pltpu.make_async_copy(g_hbm, g, load_sem.at[1]),
        pltpu.make_async_copy(gate_hbm, gate, load_sem.at[2]),
        pltpu.make_async_copy(up_hbm, up, load_sem.at[3]),
        pltpu.make_async_copy(e_hbm, e, load_sem.at[4]),
        pltpu.make_async_copy(g_hbm.at[:, cols(0, my)], gcols.at[0, tensor], load_sem.at[5]),
        pltpu.make_async_copy(g_hbm.at[:, cols(1, mx)], gcols.at[1, tensor], load_sem.at[6]),
    ]
    for load in loads:
        load.start()

    barrier = pltpu.get_barrier_semaphore()

    @pl.loop(1, TENSOR)
    def _(k):
        pl.semaphore_signal(barrier, inc=1, device_id={"tensor": lax.rem(tensor + k, TENSOR)}, device_id_type=MESH)

    @pl.loop(1, DP)
    def _(k):
        pl.semaphore_signal(barrier, inc=1, device_id={"dp": lax.rem(dp + k, DP)}, device_id_type=MESH)

    block_y = lax.rem(my + Y - lax.rem(mz, Y), Y)
    block_x = lax.rem(mx + X - lax.rem(mz, X), X)
    source = jnp.where(mz < Y, mx * Y + block_y, block_x * Y + my)
    own_source = lax.rem(mz, Y) == 0

    @pl.loop(0, Z)
    def _(z):
        @pl.when(jnp.logical_not(jnp.logical_and(own_source, z == mz)))
        def _():
            pl.semaphore_signal(
                barrier, inc=1, device_id={"dp": z * 2 + core, "tensor": source}, device_id_type=MESH
            )

    def remote(src, dst, send, recv, peer):
        return pltpu.make_async_remote_copy(
            src_ref=src, dst_ref=dst, send_sem=send, recv_sem=recv, device_id=peer, device_id_type=MESH
        )

    def y_peer(k):
        return {"tensor": mx * Y + lax.rem(my + k, Y)}

    def x_peer(k):
        return {"tensor": lax.rem(mx + k, X) * Y + my}

    def dp_peer(k):
        return {"dp": lax.rem(dp + k, DP)}

    def z_peer(k):
        return {"dp": lax.rem(mz + k, Z) * 2 + core}

    other_core = {"dp": mz * 2 + 1 - core}

    def proj_copy(k):
        return remote(
            proj, proj_in.at[tensor], proj_s.at[0], proj_r.at[0], {"tensor": lax.rem(tensor + k, TENSOR)}
        )

    def ga_copy(k):
        return remote(
            g.at[:, cols(0, lax.rem(my + k, Y))], gcols.at[0, tensor], gs_s.at[0], gs_r.at[0, k], y_peer(k)
        )

    def gb_copy(k):
        return remote(
            g.at[:, cols(1, lax.rem(mx + k, X))], gcols.at[1, tensor], gs_s.at[1], gs_r.at[1, k], x_peer(k)
        )

    def gax_copy(i, k):
        row = gcols.at[0, mx * Y + i]
        return remote(row, row, gl_s.at[0], gl_r.at[0], x_peer(k))

    def gby_copy(i, k):
        row = gcols.at[1, i * Y + my]
        return remote(row, row, gl_s.at[1], gl_r.at[1], y_peer(k))

    def lc_copy():
        rows = left.at[pl.ds((1 - core) * Z, Z)]
        return remote(rows, left_half, lc_s.at[0], lc_r.at[0], other_core)

    def ls_copy(k):
        return remote(left.at[core * Z + lax.rem(mz + k, Z)], left_in.at[k], ls_s.at[0], ls_r.at[0], z_peer(k))

    def la_copy(k):
        return remote(left_red, left_all.at[core * Z + mz], la_s.at[0], la_r.at[k], z_peer(k))

    def lf_copy(k):
        held = left_all.at[core * Z + lax.rem(mz + Z - k, Z)]
        return remote(held, held, lf_s.at[0], lf_r.at[0], other_core)

    def mixa_copy(k):
        return remote(mix.at[0, 0], mix.at[0, k], mx_s.at[0], mx_r.at[0], y_peer(k))

    def mixb_copy(k):
        return remote(mix.at[0, 0], mix.at[1, k], mx_s.at[1], mx_r.at[1], x_peer(k))

    errors_copy = remote(errors.at[1 - core], errors_in, ec_s.at[0], ec_r.at[0], other_core)

    def part_copy(half):
        return remote(part.at[1 - core, half], part_in.at[half], pc_s.at[half], pc_r.at[half], other_core)

    def chunk(z):
        return jnp.where(z < Y, lax.rem(my + Y - lax.rem(z, Y), Y), Y + lax.rem(mx + X - lax.rem(z, X), X))

    def es_copy(k):
        return remote(esum.at[chunk(lax.rem(mz + k, Z))], esum_in.at[k], es_s.at[0], es_r.at[0], z_peer(k))

    def psa_copy(k):
        peer = {"dp": k * 2 + core, "tensor": mx * Y + lax.rem(my + k, Y)}
        return remote(psum.at[0, k], psum_in.at[mz], ps_s.at[0], ps_r.at[0], peer)

    def psb_copy(k):
        peer = {"dp": (Y + k) * 2 + core, "tensor": lax.rem(mx + k, X) * Y + my}
        return remote(psum.at[1, k], psum_in.at[mz], ps_s.at[1], ps_r.at[0], peer)

    def ra_copy(k):
        return remote(red, qbuf.at[chunk(mz) * 2 + core], ra_s.at[0], ra_r.at[k], z_peer(k))

    def fw_copy(k):
        held = qbuf.at[chunk(lax.rem(mz + Z - k, Z)) * 2 + core]
        return remote(held, held, fw_s.at[0], fw_r.at[0], other_core)

    def start(copy, count):
        pl.loop(1, count)(lambda k: copy(k).start())

    def took(like, sem):
        pltpu.make_async_copy(like, like, sem).wait()

    loads[0].wait()
    sks[...] = split(sk[...])
    loads[1].wait()
    projected = fold(dot(sks[...], g[...], NT))
    high = projected.astype(BF16)
    low = (projected - high.astype(F32)).astype(BF16)
    proj[...] = jnp.concatenate([high, low], axis=1)
    proj_in[tensor] = proj[...]

    pl.semaphore_wait(barrier, TENSOR - 1 + DP - 1 + Z - own_source.astype(jnp.int32))
    start(proj_copy, TENSOR)
    start(ga_copy, Y)
    start(gb_copy, X)

    loads[5].wait()
    loads[6].wait()
    start(functools.partial(gax_copy, my), X)
    start(functools.partial(gby_copy, mx), Y)

    loads[2].wait()
    loads[3].wait()

    @pl.loop(0, TOK // 64)
    def _(j):
        rows = pl.ds(pl.multiple_of(j * 64, 64), 64)
        v = gate[rows, :].astype(F32)
        u = up[rows, :].astype(F32)
        hidden[rows, :] = (v / (1.0 + jnp.exp(-v)) * u).astype(BF16)

    loads[4].wait()
    for at in range(0, WIDTH, 256):
        to = min(at + 256, WIDTH)
        leftw[:, at:to] = fold(dot(sks[...], e[at:to, :], NT))

    took(proj_in.at[pl.ds(1, TENSOR - 1)], proj_r.at[0])
    for j in range(TENSOR // 2):
        a = proj_in[2 * j]
        b = proj_in[2 * j + 1]
        proj_all[0:R, j * 128 : (j + 1) * 128] = jnp.concatenate([a[:, :OWN], b[:, :OWN]], axis=1)
        proj_all[R : 2 * R, j * 128 : (j + 1) * 128] = jnp.concatenate([a[:, OWN:], b[:, OWN:]], axis=1)
    mine = leftw[...] + fold(dot(proj_all[...], hidden[...]))
    mine = jnp.concatenate([mine, jnp.zeros((R, 4 * LC - WIDTH), F32)], axis=1)
    for p in range(DP):
        left[p] = mine[8 * (p // 4) : 8 * (p // 4) + 8, LC * (p % 4) : LC * (p % 4) + LC]

    lc_copy().start()
    lc_copy().wait_recv()
    for j in range(Z):
        left[core * Z + j] += left_half[j]
    start(ls_copy, Z)
    @pl.loop(1, 4)
    def _(k):
        ga_copy(k).wait_recv()
        start(functools.partial(gax_copy, lax.rem(my + Y - k, Y)), X)
        gb_copy(k).wait_recv()
        start(functools.partial(gby_copy, lax.rem(mx + X - k, X)), Y)

    took(left_in.at[pl.ds(1, Z - 1)], ls_r.at[0])
    left_red[...] = left[core * Z + mz] + functools.reduce(jnp.add, [left_in[k] for k in range(1, Z)])
    start(la_copy, Z)
    left_all[core * Z + mz] = left_red[...]
    lf_copy(0).start()

    @pl.loop(1, Z)
    def _(k):
        la_copy(k).wait_recv()
        lf_copy(k).start()

    took(left_all.at[pl.ds(0, Z)], lf_r.at[0])
    for p in range(DP):
        width = min(LC, WIDTH - LC * (p % 4))
        leftw[8 * (p // 4) : 8 * (p // 4) + 8, LC * (p % 4) : LC * (p % 4) + width] = left_all[p][:, :width]

    whole = split(leftw[...])
    mixed = split(fold(dot(whole, hidden[...], NT)))
    mix[0, 0] = mixed
    start(mixa_copy, Y)
    start(mixb_copy, X)
    mix[1, 0] = mixed

    @pl.loop(0, Z)
    def _(j):
        for half in range(2):
            at = pl.multiple_of(j * 2 * CH + half * CH, CH)
            errors[half, j] = fold(dot(whole, e[:, pl.ds(at, CH)]))

    errors_copy.start()
    errors_copy.wait_recv()
    for j in range(Z):
        esum[j] = errors[core, j] + errors_in[j]
    start(es_copy, Z)

    took(gcols.at[0, pl.ds(0, 12)], gl_r.at[0])

    def product(side):
        rows = mix[side].reshape(4 * 2 * R, TOK)
        for half in range(2):
            block = dot(rows, gcols[side, :, :, half * CH : (half + 1) * CH].reshape(TOK, CH))
            for k in range(4):
                part[half, side, (4 - k) % 4] = fold(block[2 * R * k : 2 * R * (k + 1)])

    took(mix.at[0, pl.ds(1, 3)], mx_r.at[0])
    product(0)
    part_copy(0).start()
    took(gcols.at[1, pl.ds(0, 12)], gl_r.at[1])
    took(mix.at[1, pl.ds(1, 3)], mx_r.at[1])
    product(1)
    part_copy(1).start()

    def pieces(side, copy):
        part_copy(side).wait_recv()
        for k in range(4):
            psum[side, k] = part[core, side, k] + part_in[side, k]
        start(copy, 4)

        @pl.when(mz == 4 * side)
        def _():
            pltpu.make_async_copy(psum.at[side, 0], psum_in.at[mz], ps_r.at[0]).start()

        @pl.when(mz != 4 * side)
        def _():
            copy(0).start()

    pieces(0, psa_copy)
    pieces(1, psb_copy)

    full = leftw[...]
    factor = inverse_factor(dot(full, full, NT, HIGH))
    p_ref[...] = dot(factor, full, NN, HIGH) * (float(WIDTH) ** 0.5)
    took(proj_in.at[pl.ds(1, TENSOR - 1)], proj_s.at[0])
    for side in range(2):
        took(gcols.at[side, pl.ds(0, 3)], gs_s.at[side])
        took(gcols.at[side, pl.ds(0, 12)], gl_s.at[side])
        took(mix.at[side, pl.ds(1, 3)], mx_s.at[side])
        part_copy(side).wait_send()
    lc_copy().wait_send()
    took(left_in.at[pl.ds(1, Z - 1)], ls_s.at[0])
    took(left_in.at[pl.ds(1, Z - 1)], la_s.at[0])
    took(left_in, lf_s.at[0])
    errors_copy.wait_send()
    took(esum_in.at[pl.ds(1, Z - 1)], es_s.at[0])

    took(esum_in.at[pl.ds(1, Z - 1)], es_r.at[0])
    total = esum[chunk(mz)] + functools.reduce(jnp.add, [esum_in[k] for k in range(1, Z)])
    took(psum_in, ps_r.at[0])
    total = total + functools.reduce(jnp.add, [psum_in[z] for z in range(Z)])
    total = dot(factor, total, NN, HIGH) * (1.0 / (DP * float(WIDTH) ** 0.5))
    red[...] = total.astype(BF16)
    start(ra_copy, Z)
    qbuf[chunk(mz) * 2 + core] = red[...]
    fw_copy(0).start()

    @pl.loop(1, Z)
    def _(k):
        ra_copy(k).wait_recv()
        fw_copy(k).start()

    took(qbuf.at[pl.ds(0, Z)], fw_r.at[0])
    for p in range(DP):
        q_ref[:, p * CH : (p + 1) * CH] = qbuf[p].astype(F32)

    for side in range(2):
        took(psum.at[side, pl.ds(0, 3)], ps_s.at[side])

        @pl.when(mz != 4 * side)
        def _():
            took(psum.at[side, 0], ps_s.at[side])

    took(qbuf.at[pl.ds(0, Z - 1)], ra_s.at[0])
    took(qbuf.at[pl.ds(0, Z)], fw_s.at[0])


def shards(gate_pre, up_pre, grad_out, error, sketch):
    vmem = pltpu.VMEM
    dma = pltpu.SemaphoreType.DMA
    scratch = [
        vmem((TOK, WIDTH), BF16),
        vmem((TOK, WIDTH), BF16),
        vmem((TOK, WIDTH), BF16),
        vmem((OWN, D), BF16),
        vmem((WIDTH, D), BF16),
        vmem((R, D), F32),
        vmem((2 * R, D), BF16),
        vmem((2, TENSOR, OWN, COLS), BF16),
        vmem((R, 2 * OWN), BF16),
        vmem((TENSOR, R, 2 * OWN), BF16),
        vmem((2 * R, TOK), BF16),
        vmem((DP, 8, LC), F32),
        vmem((Z, 8, LC), F32),
        vmem((Z, 8, LC), F32),
        vmem((8, LC), F32),
        vmem((DP, 8, LC), F32),
        vmem((R, WIDTH), F32),
        vmem((2, 4, 2 * R, TOK), BF16),
        vmem((2, Z, R, CH), F32),
        vmem((Z, R, CH), F32),
        vmem((Z, R, CH), F32),
        vmem((Z, R, CH), F32),
        vmem((2, 2, 4, R, CH), F32),
        vmem((2, 4, R, CH), F32),
        vmem((2, 4, R, CH), F32),
        vmem((Z, R, CH), F32),
        vmem((R, CH), BF16),
        vmem((DP, R, CH), BF16),
        dma((7,)),
        dma((1,)), dma((1,)),
        dma((2,)), dma((2, 4)),
        dma((2,)), dma((2,)),
        dma((1,)), dma((1,)),
        dma((1,)), dma((1,)),
        dma((1,)), dma((Z,)),
        dma((1,)), dma((1,)),
        dma((2,)), dma((2,)),
        dma((1,)), dma((1,)),
        dma((1,)), dma((1,)),
        dma((2,)), dma((2,)),
        dma((2,)), dma((1,)),
        dma((1,)), dma((Z,)),
        dma((1,)), dma((1,)),
    ]
    p_factor, q_factor = pl.pallas_call(
        kernel,
        out_shape=(pltpu.VMEM((R, WIDTH), F32), pltpu.VMEM((R, D), F32)),
        in_specs=[pl.BlockSpec(memory_space=pl.ANY)] * 5,
        out_specs=(pl.BlockSpec(memory_space=pltpu.VMEM), pl.BlockSpec(memory_space=pltpu.VMEM)),
        scratch_shapes=scratch,
        compiler_params=pltpu.CompilerParams(
            collective_id=0, has_side_effects=True, vmem_limit_bytes=56 * 1024 * 1024
        ),
    )(gate_pre, up_pre, grad_out, error[0], sketch)
    return p_factor, q_factor[None]


def solution(mesh):
    return jax.shard_map(
        shards,
        mesh=mesh,
        in_specs=(
            P("dp", "tensor"),
            P("dp", "tensor"),
            P(("dp", "tensor"), None),
            P("dp", "tensor", None),
            P(),
        ),
        out_specs=(P(None, "tensor"), P("tensor", None, None)),
        check_vma=False,
    )
```

time: 65.1 us -> 59.3 us (0.911)
  Pallas kernels: 64.4 us -> 57.2 us
  local copies, waits for them, and re-layouts: 0 us -> 1.44 us
    pallas_call x2 -> x1, Pallas kernels: 64.4 us -> 57.2 us  [shards(): pl.pallas_call(kernel, out_shape=(pltpu.VMEM((R, WIDTH), F32), pltpu.VMEM...]
    unnamed x0 -> x2, local copies, waits for them, and re-layouts: none -> 1.44 us
where the time goes in v3:
time: 59.3 us
  Pallas kernels  57.2 us (96%)
  local copies, waits for them, and re-layouts  1.44 us (2%)
  between operations  0.64 us (1%)
    pallas_call x1, Pallas kernels, shards(): pl.pallas_call(kernel, out_shape=(pltpu.VMEM((R, WIDTH), F32), pltpu.VMEM...  57.2 us
    unnamed x2, local copies, waits for them, and re-layouts  1.44 us

profile of v3, /device:TPU:1, one launch (start us, length us, event | category | flops | bytes accessed | tf_op | source)
XLA Modules:
  0.0 59.3 jit_solution(9479276277759441794)
XLA Ops:
  0.6 57.2 %shard_map.68 = (f32[32,896]{1,0:T(8,128)S(1)}, f32[32,4096]{1,0:T(8,128)S(1)}) custom-call(bf16[1024,896]{1,0:T(8,128)(2,1)} %gate_hbm.1, bf16[1024,896]{1,0:T(8,128)(2,1)} %up_hbm.1, bf16[64,4096]{1,0:T(8,128)(2,1)} %g_hbm.1, bf16[896,4096]{1,0:T(8,128)(2,1)} %bitcast.3, f32[32,4096]{1,0:T(8,128)} %sk_hbm.1), custom_call_target="tpu_custom_call" | custom-call | tf_op jit(solution)/shard_map/pallas_call | solution.py:429
  57.8 0.6 %copy.9 = f32[32,896]{1,0:T(8,128)} copy(f32[32,896]{1,0:T(8,128)S(1)} %get-tuple-element.6) | data formatting | bytes 229376
  58.5 0.8 %copy.10 = f32[1,32,4096]{2,1,0:T(8,128)} copy(f32[1,32,4096]{2,1,0:T(8,128)S(1)} %bitcast.2) | data formatting | bytes 1048576

commit v4 on v3

--- a/solution.py
+++ b/solution.py
@@ -18,6 +18,8 @@
 WIDTH = 896
 TOK = 1024
 R = 32
+PARTS = 4
+RH = R // PARTS
 DP = 16
 TENSOR = 16
 X = 4
@@ -28,6 +30,15 @@
 COLS = HALF // 4
 CH = D // DP
 LC = 256
+RING4 = (2, 1, 3)
+RING8 = (4, 3, 5, 2, 6, 1, 7)
+GRID = tuple(
+    sorted(
+        ((a, b) for a in range(X) for b in range(Y) if a or b),
+        key=lambda k: -min(k[0], X - k[0]) - min(k[1], Y - k[1]),
+    )
+)
+LAG = 4
 
 
 def dot(a, b, dims=NN, precision=None):
@@ -133,7 +144,8 @@
 
     def proj_copy(k):
         return remote(
-            proj, proj_in.at[tensor], proj_s.at[0], proj_r.at[0], {"tensor": lax.rem(tensor + k, TENSOR)}
+            proj, proj_in.at[tensor], proj_s.at[0], proj_r.at[0],
+            {"tensor": lax.rem(mx + k[0], X) * Y + lax.rem(my + k[1], Y)},
         )
 
     def ga_copy(k):
@@ -168,30 +180,35 @@
         held = left_all.at[core * Z + lax.rem(mz + Z - k, Z)]
         return remote(held, held, lf_s.at[0], lf_r.at[0], other_core)
 
-    def mixa_copy(k):
-        return remote(mix.at[0, 0], mix.at[0, k], mx_s.at[0], mx_r.at[0], y_peer(k))
-
-    def mixb_copy(k):
-        return remote(mix.at[0, 0], mix.at[1, k], mx_s.at[1], mx_r.at[1], x_peer(k))
-
-    errors_copy = remote(errors.at[1 - core], errors_in, ec_s.at[0], ec_r.at[0], other_core)
-
-    def part_copy(half):
-        return remote(part.at[1 - core, half], part_in.at[half], pc_s.at[half], pc_r.at[half], other_core)
+    def mix_copy(half, side, k):
+        return remote(
+            mix.at[half, 0, 0], mix.at[half, side, k], mx_s.at[half, side], mx_r.at[half, side],
+            (y_peer, x_peer)[side](k),
+        )
+
+    def errors_copy(j):
+        return remote(errors.at[1 - core, j], errors_in.at[j], ec_s.at[0], ec_r.at[j], other_core)
 
     def chunk(z):
         return jnp.where(z < Y, lax.rem(my + Y - lax.rem(z, Y), Y), Y + lax.rem(mx + X - lax.rem(z, X), X))
 
-    def es_copy(k):
-        return remote(esum.at[chunk(lax.rem(mz + k, Z))], esum_in.at[k], es_s.at[0], es_r.at[0], z_peer(k))
-
-    def psa_copy(k):
-        peer = {"dp": k * 2 + core, "tensor": mx * Y + lax.rem(my + k, Y)}
-        return remote(psum.at[0, k], psum_in.at[mz], ps_s.at[0], ps_r.at[0], peer)
-
-    def psb_copy(k):
-        peer = {"dp": (Y + k) * 2 + core, "tensor": lax.rem(mx + k, X) * Y + my}
-        return remote(psum.at[1, k], psum_in.at[mz], ps_s.at[1], ps_r.at[0], peer)
+    def owner(j):
+        return jnp.where(j < Y, lax.rem(my + Y - lax.rem(j, Y), Y), Y + lax.rem(mx + X - lax.rem(j, X), X))
+
+    def es_copy(j):
+        return remote(esum.at[j], esum_in.at[mz], es_s.at[0], es_r.at[0], {"dp": owner(j) * 2 + core})
+
+    def part_copy(half, side):
+        return remote(
+            part.at[half, 1 - core, side], part_in.at[half, side], pc_s.at[half, side], pc_r.at[half, side], other_core
+        )
+
+    def ps_copy(half, side, k):
+        there = (mx * Y + lax.rem(my + k, Y), lax.rem(mx + k, X) * Y + my)[side]
+        return remote(
+            psum.at[half, side, k], psum_in.at[half, mz], ps_s.at[half, side], ps_r.at[half],
+            {"dp": (Y * side + k) * 2 + core, "tensor": there},
+        )
 
     def ra_copy(k):
         return remote(red, qbuf.at[chunk(mz) * 2 + core], ra_s.at[0], ra_r.at[k], z_peer(k))
@@ -200,8 +217,9 @@
         held = qbuf.at[chunk(lax.rem(mz + Z - k, Z)) * 2 + core]
         return remote(held, held, fw_s.at[0], fw_r.at[0], other_core)
 
-    def start(copy, count):
-        pl.loop(1, count)(lambda k: copy(k).start())
+    def start(copy, order):
+        for k in order:
+            copy(k).start()
 
     def took(like, sem):
         pltpu.make_async_copy(like, like, sem).wait()
@@ -216,14 +234,14 @@
     proj_in[tensor] = proj[...]
 
     pl.semaphore_wait(barrier, TENSOR - 1 + DP - 1 + Z - own_source.astype(jnp.int32))
-    start(proj_copy, TENSOR)
-    start(ga_copy, Y)
-    start(gb_copy, X)
+    start(proj_copy, GRID)
+    start(ga_copy, RING4)
+    start(gb_copy, RING4)
 
     loads[5].wait()
     loads[6].wait()
-    start(functools.partial(gax_copy, my), X)
-    start(functools.partial(gby_copy, mx), Y)
+    start(functools.partial(gax_copy, my), RING4)
+    start(functools.partial(gby_copy, mx), RING4)
 
     loads[2].wait()
     loads[3].wait()
@@ -255,22 +273,21 @@
     lc_copy().wait_recv()
     for j in range(Z):
         left[core * Z + j] += left_half[j]
-    start(ls_copy, Z)
+    start(ls_copy, RING8)
     @pl.loop(1, 4)
     def _(k):
         ga_copy(k).wait_recv()
-        start(functools.partial(gax_copy, lax.rem(my + Y - k, Y)), X)
+        start(functools.partial(gax_copy, lax.rem(my + Y - k, Y)), RING4)
         gb_copy(k).wait_recv()
-        start(functools.partial(gby_copy, lax.rem(mx + X - k, X)), Y)
+        start(functools.partial(gby_copy, lax.rem(mx + X - k, X)), RING4)
 
     took(left_in.at[pl.ds(1, Z - 1)], ls_r.at[0])
     left_red[...] = left[core * Z + mz] + functools.reduce(jnp.add, [left_in[k] for k in range(1, Z)])
-    start(la_copy, Z)
+    start(la_copy, RING8)
     left_all[core * Z + mz] = left_red[...]
     lf_copy(0).start()
 
-    @pl.loop(1, Z)
-    def _(k):
+    for k in reversed(RING8):
         la_copy(k).wait_recv()
         lf_copy(k).start()
 
@@ -280,57 +297,67 @@
         leftw[8 * (p // 4) : 8 * (p // 4) + 8, LC * (p % 4) : LC * (p % 4) + width] = left_all[p][:, :width]
 
     whole = split(leftw[...])
-    mixed = split(fold(dot(whole, hidden[...], NT)))
-    mix[0, 0] = mixed
-    start(mixa_copy, Y)
-    start(mixb_copy, X)
-    mix[1, 0] = mixed
-
-    @pl.loop(0, Z)
+    mixed = fold(dot(whole, hidden[...], NT))
+    for half in range(PARTS):
+        mix[half, 0, 0] = split(mixed[RH * half : RH * (half + 1)])
+        for side in range(2):
+            start(functools.partial(mix_copy, half, side), RING4)
+    for half in range(PARTS):
+        mix[half, 1, 0] = mix[half, 0, 0]
+
+    @pl.loop(0, Z + LAG)
     def _(j):
-        for half in range(2):
-            at = pl.multiple_of(j * 2 * CH + half * CH, CH)
-            errors[half, j] = fold(dot(whole, e[:, pl.ds(at, CH)]))
-
-    errors_copy.start()
-    errors_copy.wait_recv()
-    for j in range(Z):
-        esum[j] = errors[core, j] + errors_in[j]
-    start(es_copy, Z)
-
-    took(gcols.at[0, pl.ds(0, 12)], gl_r.at[0])
-
-    def product(side):
-        rows = mix[side].reshape(4 * 2 * R, TOK)
-        for half in range(2):
-            block = dot(rows, gcols[side, :, :, half * CH : (half + 1) * CH].reshape(TOK, CH))
+        @pl.when(j < Z)
+        def _():
+            for part_of in range(2):
+                at = pl.multiple_of(j * 2 * CH + part_of * CH, CH)
+                errors[part_of, j] = fold(dot(whole, e[:, pl.ds(at, CH)]))
+            errors_copy(j).start()
+
+        @pl.when(j >= LAG)
+        def _():
+            i = j - LAG
+            errors_copy(i).wait_recv()
+            esum[i] = errors[core, i] + errors_in[i]
+
+            @pl.when(owner(i) == mz)
+            def _():
+                esum_in[mz] = esum[i]
+
+            @pl.when(owner(i) != mz)
+            def _():
+                es_copy(i).start()
+
+    def product(half, side):
+        took(mix.at[half, side, pl.ds(1, 3)], mx_r.at[half, side])
+        rows = mix[half, side].reshape(4 * 2 * RH, TOK)
+        for part_of in range(2):
+            block = dot(rows, gcols[side, :, :, part_of * CH : (part_of + 1) * CH].reshape(TOK, CH))
             for k in range(4):
-                part[half, side, (4 - k) % 4] = fold(block[2 * R * k : 2 * R * (k + 1)])
-
-    took(mix.at[0, pl.ds(1, 3)], mx_r.at[0])
-    product(0)
-    part_copy(0).start()
-    took(gcols.at[1, pl.ds(0, 12)], gl_r.at[1])
-    took(mix.at[1, pl.ds(1, 3)], mx_r.at[1])
-    product(1)
-    part_copy(1).start()
-
-    def pieces(side, copy):
-        part_copy(side).wait_recv()
+                part[half, part_of, side, (4 - k) % 4] = fold(block[2 * RH * k : 2 * RH * (k + 1)])
+        part_copy(half, side).start()
+
+    def pieces(half, side):
+        part_copy(half, side).wait_recv()
         for k in range(4):
-            psum[side, k] = part[core, side, k] + part_in[side, k]
-        start(copy, 4)
+            psum[half, side, k] = part[half, core, side, k] + part_in[half, side, k]
+        start(functools.partial(ps_copy, half, side), RING4)
 
         @pl.when(mz == 4 * side)
         def _():
-            pltpu.make_async_copy(psum.at[side, 0], psum_in.at[mz], ps_r.at[0]).start()
+            pltpu.make_async_copy(psum.at[half, side, 0], psum_in.at[half, mz], ps_r.at[half]).start()
 
         @pl.when(mz != 4 * side)
         def _():
-            copy(0).start()
-
-    pieces(0, psa_copy)
-    pieces(1, psb_copy)
+            ps_copy(half, side, 0).start()
+
+    for side in range(2):
+        took(gcols.at[side, pl.ds(0, 12)], gl_r.at[side])
+    for half in range(PARTS):
+        for side in range(2):
+            product(half, side)
+        for side in range(2):
+            pieces(half, side)
 
     full = leftw[...]
     factor = inverse_factor(dot(full, full, NT, HIGH))
@@ -339,27 +366,30 @@
     for side in range(2):
         took(gcols.at[side, pl.ds(0, 3)], gs_s.at[side])
         took(gcols.at[side, pl.ds(0, 12)], gl_s.at[side])
-        took(mix.at[side, pl.ds(1, 3)], mx_s.at[side])
-        part_copy(side).wait_send()
+        for half in range(PARTS):
+            took(mix.at[half, side, pl.ds(1, 3)], mx_s.at[half, side])
+            part_copy(half, side).wait_send()
     lc_copy().wait_send()
     took(left_in.at[pl.ds(1, Z - 1)], ls_s.at[0])
     took(left_in.at[pl.ds(1, Z - 1)], la_s.at[0])
     took(left_in, lf_s.at[0])
-    errors_copy.wait_send()
+    took(errors_in, ec_s.at[0])
     took(esum_in.at[pl.ds(1, Z - 1)], es_s.at[0])
 
     took(esum_in.at[pl.ds(1, Z - 1)], es_r.at[0])
-    total = esum[chunk(mz)] + functools.reduce(jnp.add, [esum_in[k] for k in range(1, Z)])
-    took(psum_in, ps_r.at[0])
-    total = total + functools.reduce(jnp.add, [psum_in[z] for z in range(Z)])
+    total = functools.reduce(jnp.add, [esum_in[z] for z in range(Z)])
+    for half in range(PARTS):
+        took(psum_in.at[half], ps_r.at[half])
+    total = total + jnp.concatenate(
+        [functools.reduce(jnp.add, [psum_in[half, z] for z in range(Z)]) for half in range(PARTS)], axis=0
+    )
     total = dot(factor, total, NN, HIGH) * (1.0 / (DP * float(WIDTH) ** 0.5))
     red[...] = total.astype(BF16)
-    start(ra_copy, Z)
+    start(ra_copy, RING8)
     qbuf[chunk(mz) * 2 + core] = red[...]
     fw_copy(0).start()
 
-    @pl.loop(1, Z)
-    def _(k):
+    for k in reversed(RING8):
         ra_copy(k).wait_recv()
         fw_copy(k).start()
 
@@ -367,15 +397,24 @@
     for p in range(DP):
         q_ref[:, p * CH : (p + 1) * CH] = qbuf[p].astype(F32)
 
-    for side in range(2):
-        took(psum.at[side, pl.ds(0, 3)], ps_s.at[side])
-
-        @pl.when(mz != 4 * side)
-        def _():
-            took(psum.at[side, 0], ps_s.at[side])
+    for half in range(PARTS):
+        for side in range(2):
+            took(psum.at[half, side, pl.ds(0, 3)], ps_s.at[half, side])
+
+            @pl.when(mz != 4 * side)
+            def _():
+                took(psum.at[half, side, 0], ps_s.at[half, side])
 
     took(qbuf.at[pl.ds(0, Z - 1)], ra_s.at[0])
     took(qbuf.at[pl.ds(0, Z)], fw_s.at[0])
+
+
+def finish(p_in, q_in, p_out, q_out, sem):
+    copies = [pltpu.make_async_copy(p_in, p_out, sem.at[0]), pltpu.make_async_copy(q_in, q_out.at[0], sem.at[1])]
+    for copy in copies:
+        copy.start()
+    for copy in copies:
+        copy.wait()
 
 
 def shards(gate_pre, up_pre, grad_out, error, sketch):
@@ -399,15 +438,15 @@
         vmem((8, LC), F32),
         vmem((DP, 8, LC), F32),
         vmem((R, WIDTH), F32),
-        vmem((2, 4, 2 * R, TOK), BF16),
+        vmem((PARTS, 2, 4, 2 * RH, TOK), BF16),
         vmem((2, Z, R, CH), F32),
         vmem((Z, R, CH), F32),
         vmem((Z, R, CH), F32),
         vmem((Z, R, CH), F32),
-        vmem((2, 2, 4, R, CH), F32),
-        vmem((2, 4, R, CH), F32),
-        vmem((2, 4, R, CH), F32),
-        vmem((Z, R, CH), F32),
+        vmem((PARTS, 2, 2, 4, RH, CH), F32),
+        vmem((PARTS, 2, 4, RH, CH), F32),
+        vmem((PARTS, 2, 4, RH, CH), F32),
+        vmem((PARTS, Z, RH, CH), F32),
         vmem((R, CH), BF16),
         vmem((DP, R, CH), BF16),
         dma((7,)),
@@ -418,11 +457,11 @@
         dma((1,)), dma((1,)),
         dma((1,)), dma((Z,)),
         dma((1,)), dma((1,)),
-        dma((2,)), dma((2,)),
+        dma((PARTS, 2)), dma((PARTS, 2)),
+        dma((1,)), dma((Z,)),
         dma((1,)), dma((1,)),
-        dma((1,)), dma((1,)),
-        dma((2,)), dma((2,)),
-        dma((2,)), dma((1,)),
+        dma((PARTS, 2)), dma((PARTS, 2)),
+        dma((PARTS, 2)), dma((PARTS,)),
         dma((1,)), dma((Z,)),
         dma((1,)), dma((1,)),
     ]
@@ -436,7 +475,13 @@
             collective_id=0, has_side_effects=True, vmem_limit_bytes=56 * 1024 * 1024
         ),
     )(gate_pre, up_pre, grad_out, error[0], sketch)
-    return p_factor, q_factor[None]
+    return pl.pallas_call(
+        finish,
+        out_shape=(jax.ShapeDtypeStruct((R, WIDTH), F32), jax.ShapeDtypeStruct((1, R, D), F32)),
+        in_specs=[pl.BlockSpec(memory_space=pltpu.VMEM)] * 2,
+        out_specs=(pl.BlockSpec(memory_space=pl.ANY), pl.BlockSpec(memory_space=pl.ANY)),
+        scratch_shapes=[dma((2,))],
+    )(pltpu.with_memory_space_constraint(p_factor, pltpu.VMEM), pltpu.with_memory_space_constraint(q_factor, pltpu.VMEM))
 
 
 def solution(mesh):

time: 59.3 us -> 56.8 us (0.958)
  local copies, waits for them, and re-layouts: 1.44 us -> 0 us
  Pallas kernels: 57.2 us -> 56.1 us
    pallas_call x1, Pallas kernels: 57.2 us -> 55.2 us  [shards(): pl.pallas_call(kernel, out_shape=(pltpu.VMEM((R, WIDTH), F32), pltpu.VMEM...]
    unnamed x2 -> x0, local copies, waits for them, and re-layouts: 1.44 us -> none
    pallas_call x0 -> x1, Pallas kernels: none -> 0.85 us  [shards(): pl.pallas_call(finish, out_shape=(jax.ShapeDtypeStruct((R, WIDTH), F32),...]
where the time goes in v4:
time: 56.8 us; the launch traced here: 56.7 us
  Pallas kernels  56.1 us (99%)
  between operations  0.64 us (1%)
    pallas_call x1, Pallas kernels, shards(): pl.pallas_call(kernel, out_shape=(pltpu.VMEM((R, WIDTH), F32), pltpu.VMEM...  55.2 us

profile of v4, /device:TPU:1, one launch (start us, length us, event | category | flops | bytes accessed | tf_op | source)
XLA Modules:
  0.0 56.7 jit_solution(325431346565324568)
XLA Ops:
  0.6 55.2 %shard_map.68 = (f32[32,896]{1,0:T(8,128)S(1)}, f32[32,4096]{1,0:T(8,128)S(1)}) custom-call(bf16[1024,896]{1,0:T(8,128)(2,1)} %gate_hbm.1, bf16[1024,896]{1,0:T(8,128)(2,1)} %up_hbm.1, bf16[64,4096]{1,0:T(8,128)(2,1)} %g_hbm.1, bf16[896,4096]{1,0:T(8,128)(2,1)} %bitcast.1, f32[32,4096]{1,0:T(8,128)} %sk_hbm.1), custom_call_target="tpu_custom_call" | custom-call | tf_op jit(solution)/shard_map/pallas_call | solution.py:468
  55.9 0.9 %shard_map.69 = (f32[32,896]{1,0:T(8,128)}, f32[1,32,4096]{2,1,0:T(8,128)}) custom-call(f32[32,896]{1,0:T(8,128)S(1)} %get-tuple-element.4.p_in, f32[32,4096]{1,0:T(8,128)S(1)} %get-tuple-element.5.q_in), custom_call_target="tpu_custom_call" | custom-call | tf_op jit(solution)/shard_map/pallas_call | solution.py:478

commit v5 on v4

v5 whole, which is shorter than its diff:
```python
import functools

import jax
import jax.numpy as jnp
from jax import lax
from jax.experimental import pallas as pl
from jax.experimental.pallas import tpu as pltpu
from jax.sharding import PartitionSpec as P

MESH = pl.DeviceIdType.MESH
HIGH = lax.Precision.HIGHEST
F32 = jnp.float32
BF16 = jnp.bfloat16
NT = (((1,), (1,)), ((), ()))
NN = (((1,), (0,)), ((), ()))

D = 4096
WIDTH = 896
TOK = 1024
R = 32
PARTS = 4
RH = R // PARTS
DP = 16
TENSOR = 16
X = 4
Y = 4
Z = 8
OWN = 64
HALF = D // 2
COLS = HALF // 4
CH = D // DP
LC = 256
RING4 = (2, 1, 3)
RING8 = (4, 3, 5, 2, 6, 1, 7)
GRID = tuple(
    sorted(
        ((a, b) for a in range(X) for b in range(Y) if a or b),
        key=lambda k: -min(k[0], X - k[0]) - min(k[1], Y - k[1]),
    )
)
LAG = 2


def dot(a, b, dims=NN, precision=None):
    return lax.dot_general(a, b, dims, precision=precision, preferred_element_type=F32)


def split(value):
    high = value.astype(BF16)
    low = (value - high.astype(F32)).astype(BF16)
    return jnp.concatenate([high, low], axis=0)


def fold(product):
    half = product.shape[0] // 2
    return product[:half] + product[half:]


def inverse_factor(gram):
    rows = lax.broadcasted_iota(jnp.int32, (R, 128), 0)
    lanes = lax.broadcasted_iota(jnp.int32, (R, 128), 1)
    wide = jnp.concatenate([gram, jnp.zeros((R, 128 - R), F32)], axis=1)
    wide = jnp.where(lanes == rows + R, 1.0, wide)
    for k in range(R):
        factor = wide[:, k : k + 1] / wide[k : k + 1, k : k + 1]
        wide = wide - jnp.where(rows > k, factor * wide[k : k + 1, :], 0.0)
    pivots = jnp.sum(jnp.where(lanes == rows, wide, 0.0), axis=1, keepdims=True)
    return (wide * lax.rsqrt(pivots))[:, R : 2 * R]


def kernel(
    gate_hbm, up_hbm, g_hbm, e_hbm, sk_hbm,
    p_ref, q_ref,
    gate, up, hidden, g, e, sk, sks, gcols,
    proj, proj_in, proj_all, left, left_half, left_in, left_red, left_all, leftw,
    mix, errors, errors_in, esum, esum_in, part, part_in, psum, psum_in, red, qbuf,
    load_sem,
    proj_s, proj_r, gs_s, gs_r, gl_s, gl_r, lc_s, lc_r, ls_s, ls_r, la_s, la_r, lf_s, lf_r,
    mx_s, mx_r, ec_s, ec_r, es_s, es_r, pc_s, pc_r, ps_s, ps_r, ra_s, ra_r, fw_s, fw_r,
):
    dp = lax.axis_index("dp")
    tensor = lax.axis_index("tensor")
    mx = tensor // Y
    my = lax.rem(tensor, Y)
    mz = dp // 2
    core = lax.rem(dp, 2)

    barrier = pltpu.get_barrier_semaphore()

    def signal(peer):
        pl.semaphore_signal(barrier, inc=1, device_id=peer, device_id_type=MESH)

    for a, b in GRID:
        signal({"tensor": lax.rem(mx + a, X) * Y + lax.rem(my + b, Y)})

    def cols(half, place):
        return pl.ds(pl.multiple_of(half * HALF + place * COLS, COLS), COLS)

    loads = [
        pltpu.make_async_copy(sk_hbm, sk, load_sem.at[0]),
        pltpu.make_async_copy(g_hbm, g, load_sem.at[1]),
        pltpu.make_async_copy(gate_hbm, gate, load_sem.at[2]),
        pltpu.make_async_copy(up_hbm, up, load_sem.at[3]),
        pltpu.make_async_copy(e_hbm, e, load_sem.at[4]),
    ]
    for load in loads:
        load.start()

    for k in RING8:
        for other in (core, 1 - core):
            signal({"dp": lax.rem(mz + k, Z) * 2 + other})
    signal({"dp": mz * 2 + 1 - core})

    block_y = lax.rem(my + Y - lax.rem(mz, Y), Y)
    block_x = lax.rem(mx + X - lax.rem(mz, X), X)
    source = jnp.where(mz < Y, mx * Y + block_y, block_x * Y + my)
    own_source = lax.rem(mz, Y) == 0
    for k in RING8:
        signal({"dp": lax.rem(mz + k, Z) * 2 + core, "tensor": source})

    @pl.when(jnp.logical_not(own_source))
    def _():
        signal({"dp": dp, "tensor": source})

    def remote(src, dst, send, recv, peer):
        return pltpu.make_async_remote_copy(
            src_ref=src, dst_ref=dst, send_sem=send, recv_sem=recv, device_id=peer, device_id_type=MESH
        )

    def y_peer(k):
        return {"tensor": mx * Y + lax.rem(my + k, Y)}

    def x_peer(k):
        return {"tensor": lax.rem(mx + k, X) * Y + my}

    def dp_peer(k):
        return {"dp": lax.rem(dp + k, DP)}

    def z_peer(k):
        return {"dp": lax.rem(mz + k, Z) * 2 + core}

    other_core = {"dp": mz * 2 + 1 - core}

    def proj_copy(k):
        return remote(
            proj, proj_in.at[tensor], proj_s.at[0], proj_r.at[0],
            {"tensor": lax.rem(mx + k[0], X) * Y + lax.rem(my + k[1], Y)},
        )

    def ga_copy(k):
        return remote(
            g.at[:, cols(0, lax.rem(my + k, Y))], gcols.at[0, tensor], gs_s.at[0], gs_r.at[0], y_peer(k)
        )

    def gb_copy(k):
        return remote(
            g.at[:, cols(1, lax.rem(mx + k, X))], gcols.at[1, tensor], gs_s.at[0], gs_r.at[1], x_peer(k)
        )

    def gax_copy(i, k):
        row = gcols.at[0, mx * Y + i]
        return remote(row, row, gl_s.at[0], gl_r.at[0], x_peer(k))

    def gby_copy(i, k):
        row = gcols.at[1, i * Y + my]
        return remote(row, row, gl_s.at[0], gl_r.at[1], y_peer(k))

    def own_a():
        return g.at[:, cols(0, my)], gcols.at[0, tensor]

    def own_b():
        return g.at[:, cols(1, mx)], gcols.at[1, tensor]

    def oax_copy(k):
        return remote(*own_a(), gl_s.at[0], gl_r.at[0], x_peer(k))

    def oby_copy(k):
        return remote(*own_b(), gl_s.at[0], gl_r.at[1], y_peer(k))

    def lc_copy():
        rows = left.at[pl.ds((1 - core) * Z, Z)]
        return remote(rows, left_half, lc_s.at[0], lc_r.at[0], other_core)

    def ls_copy(k):
        return remote(left.at[core * Z + lax.rem(mz + k, Z)], left_in.at[k], ls_s.at[0], ls_r.at[0], z_peer(k))

    def la_copy(k):
        return remote(left_red, left_all.at[core * Z + mz], la_s.at[0], la_r.at[min(k, Z - k) - 1], z_peer(k))

    def lf_copy(k):
        held = left_all.at[core * Z + lax.rem(mz + Z - k, Z)]
        return remote(held, held, lf_s.at[0], lf_r.at[0], other_core)

    def mix_copy(half, side, k):
        return remote(
            mix.at[half, 0, 0], mix.at[half, side, k], mx_s.at[0], mx_r.at[half],
            (y_peer, x_peer)[side](k),
        )

    def errors_copy(j):
        pair = pl.ds(2 * j, 2)
        return remote(errors.at[1 - core, pair], errors_in.at[pair], ec_s.at[0], ec_r.at[j], other_core)

    def chunk(z):
        return jnp.where(z < Y, lax.rem(my + Y - lax.rem(z, Y), Y), Y + lax.rem(mx + X - lax.rem(z, X), X))

    def es_copy(n, z):
        return remote(esum.at[n], esum_in.at[mz], es_s.at[0], es_r.at[0], {"dp": z * 2 + core})

    def part_copy(half):
        return remote(part.at[half, 1 - core], part_in.at[half], pc_s.at[0], pc_r.at[half], other_core)

    def ps_copy(half, z):
        k = lax.rem(z, 4)
        there = jnp.where(z < 4, mx * Y + lax.rem(my + k, Y), lax.rem(mx + k, X) * Y + my)
        return remote(
            psum.at[half, z], psum_in.at[half, mz], ps_s.at[0], ps_r.at[0], {"dp": z * 2 + core, "tensor": there}
        )

    def ra_copy(k):
        return remote(red, qbuf.at[chunk(mz) * 2 + core], ra_s.at[0], ra_r.at[min(k, Z - k) - 1], z_peer(k))

    def fw_copy(k):
        held = qbuf.at[chunk(lax.rem(mz + Z - k, Z)) * 2 + core]
        return remote(held, held, fw_s.at[0], fw_r.at[0], other_core)

    def start(copy, order):
        for k in order:
            copy(k).start()

    def took(like, sem):
        pltpu.make_async_copy(like, like, sem).wait()

    loads[0].wait()
    sks[...] = split(sk[...])
    loads[1].wait()
    projected = fold(dot(sks[...], g[...], NT))
    high = projected.astype(BF16)
    low = (projected - high.astype(F32)).astype(BF16)
    proj[...] = jnp.concatenate([high, low], axis=1)
    proj_in[tensor] = proj[...]

    pl.semaphore_wait(barrier, TENSOR - 1 + DP - 1 + Z - own_source.astype(jnp.int32))
    start(proj_copy, GRID)
    start(ga_copy, RING4)
    start(gb_copy, RING4)

    start(oax_copy, RING4)
    start(oby_copy, RING4)
    pltpu.make_async_copy(*own_a(), gl_r.at[0]).start()
    pltpu.make_async_copy(*own_b(), gl_r.at[1]).start()

    loads[2].wait()
    loads[3].wait()

    @pl.loop(0, TOK // 64)
    def _(j):
        rows = pl.ds(pl.multiple_of(j * 64, 64), 64)
        v = gate[rows, :].astype(F32)
        u = up[rows, :].astype(F32)
        hidden[rows, :WIDTH] = (v / (1.0 + jnp.exp(-v)) * u).astype(BF16)
        hidden[rows, WIDTH:] = jnp.zeros((64, 4 * LC - WIDTH), BF16)

    loads[4].wait()
    for at in range(0, WIDTH, 256):
        to = min(at + 256, WIDTH)
        leftw[:, at:to] = fold(dot(sks[...], e[at:to, :], NT))

    took(proj_in.at[pl.ds(1, TENSOR - 1)], proj_r.at[0])
    for j in range(TENSOR // 2):
        a = proj_in[2 * j]
        b = proj_in[2 * j + 1]
        proj_all[0:R, j * 128 : (j + 1) * 128] = jnp.concatenate([a[:, :OWN], b[:, :OWN]], axis=1)
        proj_all[R : 2 * R, j * 128 : (j + 1) * 128] = jnp.concatenate([a[:, OWN:], b[:, OWN:]], axis=1)
    mine = leftw[:, :WIDTH] + fold(dot(proj_all[...], hidden[:, :WIDTH]))
    mine = jnp.concatenate([mine, jnp.zeros((R, 4 * LC - WIDTH), F32)], axis=1)
    for p in range(DP):
        row, at = 8 * (p % Z // 2), 2 * LC * (p // Z) + LC * (p % 2)
        left[p] = mine[row : row + 8, at : at + LC]

    lc_copy().start()
    lc_copy().wait_recv()
    for j in range(Z):
        left[core * Z + j] += left_half[j]
    start(ls_copy, RING8)
    took(gcols.at[0, pl.ds(0, 3)], gs_r.at[0])
    for k in range(1, 4):
        start(functools.partial(gax_copy, lax.rem(my + Y - k, Y)), RING4)
    took(gcols.at[1, pl.ds(0, 3)], gs_r.at[1])
    for k in range(1, 4):
        start(functools.partial(gby_copy, lax.rem(mx + X - k, X)), RING4)

    took(left_in.at[pl.ds(1, Z - 1)], ls_r.at[0])
    left_red[...] = left[core * Z + mz] + functools.reduce(jnp.add, [left_in[k] for k in range(1, Z)])
    start(la_copy, RING8)
    left_all[core * Z + mz] = left_red[...]
    lf_copy(0).start()

    for near in range(1, 5):
        pair = sorted({near, Z - near})
        took(left_all.at[pl.ds(0, len(pair))], la_r.at[near - 1])
        for k in pair:
            lf_copy(k).start()

    def product_of(which):
        chunks = [left_all[which * Z + z] for z in range(Z)]
        value = jnp.concatenate(
            [jnp.concatenate(chunks[2 * i : 2 * i + 2], axis=1) for i in range(Z // 2)], axis=0
        )
        place = pl.ds(pl.multiple_of(which * 2 * LC, 2 * LC), 2 * LC)
        leftw[:, place] = value
        return fold(dot(split(value), hidden[:, place], NT))

    mixed = product_of(core)
    took(left_all.at[pl.ds(0, Z)], lf_r.at[0])
    mixed = mixed + product_of(1 - core)
    for half in range(PARTS):
        mix[half, 0, 0] = split(mixed[RH * half : RH * (half + 1)])
        for side in range(2):
            start(functools.partial(mix_copy, half, side), RING4)
    for half in range(PARTS):
        mix[half, 1, 0] = mix[half, 0, 0]

    whole = split(leftw[:, :WIDTH])

    @pl.loop(0, Z // 2 + LAG)
    def _(j):
        @pl.when(j < Z // 2)
        def _():
            for i, offset in enumerate((4 + j, 3 - j)):
                place = chunk(lax.rem(mz + offset, Z))
                for part_of in range(2):
                    at = pl.multiple_of((2 * place + part_of) * CH, CH)
                    errors[part_of, 2 * j + i] = fold(dot(whole, e[:, pl.ds(at, CH)]))
            errors_copy(j).start()

        @pl.when(j >= LAG)
        def _():
            errors_copy(j - LAG).wait_recv()
            for i, offset in enumerate((4 + (j - LAG), 3 - (j - LAG))):
                n = 2 * (j - LAG) + i
                esum[n] = errors[core, n] + errors_in[n]

                @pl.when(offset == 0)
                def _():
                    esum_in[mz] = esum[n]

                @pl.when(offset != 0)
                def _():
                    es_copy(n, lax.rem(mz + offset, Z)).start()

    gcols_like = gcols.reshape(2 * TENSOR, OWN, COLS)
    mix_like = mix.reshape(PARTS * 2 * 4, 2 * RH, TOK)

    def product(half, side):
        rows = mix[half, side].reshape(4 * 2 * RH, TOK)
        for part_of in range(2):
            block = dot(rows, gcols[side, :, :, part_of * CH : (part_of + 1) * CH].reshape(TOK, CH))
            for k in range(4):
                part[half, part_of, side, (4 - k) % 4] = fold(block[2 * RH * k : 2 * RH * (k + 1)])

    def pieces(half):
        for side in range(2):
            for k in range(4):
                psum[half, 4 * side + k] = part[half, core, side, k] + part_in[half, side, k]
        for offset in RING8:
            ps_copy(half, lax.rem(mz + offset, Z)).start()

        @pl.when(own_source)
        def _():
            pltpu.make_async_copy(psum.at[half, mz], psum_in.at[half, mz], ps_r.at[0]).start()

        @pl.when(jnp.logical_not(own_source))
        def _():
            ps_copy(half, mz).start()

    for side in range(2):
        took(gcols.at[side, pl.ds(0, 13)], gl_r.at[side])
    for half in range(PARTS + 1):
        if half < PARTS:
            took(mix_like.at[pl.ds(0, 6)], mx_r.at[half])
            for side in range(2):
                product(half, side)
            part_copy(half).start()
        if half > 0:
            part_copy(half - 1).wait_recv()
            pieces(half - 1)

    full = leftw[:, :WIDTH]
    factor = inverse_factor(dot(full, full, NT, HIGH))
    p_ref[...] = dot(factor, full, NN, HIGH) * (float(WIDTH) ** 0.5)
    took(proj_in.at[pl.ds(1, TENSOR - 1)], proj_s.at[0])
    took(gcols_like.at[pl.ds(0, 6)], gs_s.at[0])
    took(gcols_like.at[pl.ds(0, 24)], gl_s.at[0])
    took(mix_like.at[pl.ds(0, 6 * PARTS)], mx_s.at[0])
    lc_copy().wait_send()
    took(left_in.at[pl.ds(1, Z - 1)], ls_s.at[0])
    took(left_in.at[pl.ds(1, Z - 1)], la_s.at[0])
    took(left_in, lf_s.at[0])
    took(errors_in, ec_s.at[0])
    took(esum_in.at[pl.ds(1, Z - 1)], es_s.at[0])
    took(part_in, pc_s.at[0])

    took(esum_in.at[pl.ds(1, Z - 1)], es_r.at[0])
    total = functools.reduce(jnp.add, [esum_in[z] for z in range(Z)])
    took(psum_in, ps_r.at[0])
    total = total + jnp.concatenate(
        [functools.reduce(jnp.add, [psum_in[half, z] for z in range(Z)]) for half in range(PARTS)], axis=0
    )
    total = dot(factor, total, NN, HIGH) * (1.0 / (DP * float(WIDTH) ** 0.5))
    red[...] = total.astype(BF16)
    start(ra_copy, RING8)
    qbuf[chunk(mz) * 2 + core] = red[...]
    fw_copy(0).start()

    for near in range(1, 5):
        pair = sorted({near, Z - near})
        took(qbuf.at[pl.ds(0, len(pair))], ra_r.at[near - 1])
        for k in pair:
            fw_copy(k).start()

    took(qbuf.at[pl.ds(0, Z)], fw_r.at[0])
    for p in range(DP):
        q_ref[:, p * CH : (p + 1) * CH] = qbuf[p].astype(F32)

    psum_like = psum.reshape(PARTS * Z, RH, CH)

    @pl.when(own_source)
    def _():
        took(psum_like.at[pl.ds(0, 7 * PARTS)], ps_s.at[0])

    @pl.when(jnp.logical_not(own_source))
    def _():
        took(psum_like, ps_s.at[0])

    took(qbuf.at[pl.ds(0, Z - 1)], ra_s.at[0])
    took(qbuf.at[pl.ds(0, Z)], fw_s.at[0])


def finish(p_in, q_in, p_out, q_out, sem):
    copies = [pltpu.make_async_copy(p_in, p_out, sem.at[0]), pltpu.make_async_copy(q_in, q_out.at[0], sem.at[1])]
    for copy in copies:
        copy.start()
    for copy in copies:
        copy.wait()


def shards(gate_pre, up_pre, grad_out, error, sketch):
    vmem = pltpu.VMEM
    dma = pltpu.SemaphoreType.DMA
    scratch = [
        vmem((TOK, WIDTH), BF16),
        vmem((TOK, WIDTH), BF16),
        vmem((TOK, 4 * LC), BF16),
        vmem((OWN, D), BF16),
        vmem((WIDTH, D), BF16),
        vmem((R, D), F32),
        vmem((2 * R, D), BF16),
        vmem((2, TENSOR, OWN, COLS), BF16),
        vmem((R, 2 * OWN), BF16),
        vmem((TENSOR, R, 2 * OWN), BF16),
        vmem((2 * R, TOK), BF16),
        vmem((DP, 8, LC), F32),
        vmem((Z, 8, LC), F32),
        vmem((Z, 8, LC), F32),
        vmem((8, LC), F32),
        vmem((DP, 8, LC), F32),
        vmem((R, 4 * LC), F32),
        vmem((PARTS, 2, 4, 2 * RH, TOK), BF16),
        vmem((2, Z, R, CH), F32),
        vmem((Z, R, CH), F32),
        vmem((Z, R, CH), F32),
        vmem((Z, R, CH), F32),
        vmem((PARTS, 2, 2, 4, RH, CH), F32),
        vmem((PARTS, 2, 4, RH, CH), F32),
        vmem((PARTS, Z, RH, CH), F32),
        vmem((PARTS, Z, RH, CH), F32),
        vmem((R, CH), BF16),
        vmem((DP, R, CH), BF16),
        dma((5,)),
        dma((1,)), dma((1,)),
        dma((1,)), dma((2,)),
        dma((1,)), dma((2,)),
        dma((1,)), dma((1,)),
        dma((1,)), dma((1,)),
        dma((1,)), dma((4,)),
        dma((1,)), dma((1,)),
        dma((1,)), dma((PARTS,)),
        dma((1,)), dma((Z // 2,)),
        dma((1,)), dma((1,)),
        dma((1,)), dma((PARTS,)),
        dma((1,)), dma((1,)),
        dma((1,)), dma((4,)),
        dma((1,)), dma((1,)),
    ]
    p_factor, q_factor = pl.pallas_call(
        kernel,
        out_shape=(pltpu.VMEM((R, WIDTH), F32), pltpu.VMEM((R, D), F32)),
        in_specs=[pl.BlockSpec(memory_space=pl.ANY)] * 5,
        out_specs=(pl.BlockSpec(memory_space=pltpu.VMEM), pl.BlockSpec(memory_space=pltpu.VMEM)),
        scratch_shapes=scratch,
        compiler_params=pltpu.CompilerParams(
            collective_id=0, has_side_effects=True, vmem_limit_bytes=56 * 1024 * 1024
        ),
    )(gate_pre, up_pre, grad_out, error[0], sketch)
    return pl.pallas_call(
        finish,
        out_shape=(jax.ShapeDtypeStruct((R, WIDTH), F32), jax.ShapeDtypeStruct((1, R, D), F32)),
        in_specs=[pl.BlockSpec(memory_space=pltpu.VMEM)] * 2,
        out_specs=(pl.BlockSpec(memory_space=pl.ANY), pl.BlockSpec(memory_space=pl.ANY)),
        scratch_shapes=[dma((2,))],
    )(pltpu.with_memory_space_constraint(p_factor, pltpu.VMEM), pltpu.with_memory_space_constraint(q_factor, pltpu.VMEM))


def solution(mesh):
    return jax.shard_map(
        shards,
        mesh=mesh,
        in_specs=(
            P("dp", "tensor"),
            P("dp", "tensor"),
            P(("dp", "tensor"), None),
            P("dp", "tensor", None),
            P(),
        ),
        out_specs=(P(None, "tensor"), P("tensor", None, None)),
        check_vma=False,
    )
```

time: 56.8 us -> 54.9 us (0.967)
  Pallas kernels: 56.1 us -> 54.2 us
    pallas_call x1, Pallas kernels: 55.2 us -> 53.4 us  [shards(): pl.pallas_call(kernel, out_shape=(pltpu.VMEM((R, WIDTH), F32), pltpu.VMEM...]
where the time goes in v5:
time: 54.9 us; the launch traced here: 54.8 us
  Pallas kernels  54.2 us (99%)
  between operations  0.64 us (1%)
    pallas_call x1, Pallas kernels, shards(): pl.pallas_call(kernel, out_shape=(pltpu.VMEM((R, WIDTH), F32), pltpu.VMEM...  53.4 us

profile of v5, /device:TPU:1, one launch (start us, length us, event | category | flops | bytes accessed | tf_op | source)
XLA Modules:
  0.0 54.8 jit_solution(15625109692011403281)
XLA Ops:
  0.6 53.4 %shard_map.68 = (f32[32,896]{1,0:T(8,128)S(1)}, f32[32,4096]{1,0:T(8,128)S(1)}) custom-call(bf16[1024,896]{1,0:T(8,128)(2,1)} %gate_hbm.1, bf16[1024,896]{1,0:T(8,128)(2,1)} %up_hbm.1, bf16[64,4096]{1,0:T(8,128)(2,1)} %g_hbm.1, bf16[896,4096]{1,0:T(8,128)(2,1)} %bitcast.1, f32[32,4096]{1,0:T(8,128)} %sk_hbm.1), custom_call_target="tpu_custom_call" | custom-call | tf_op jit(solution)/shard_map/pallas_call | solution.py:496
  54.0 0.9 %shard_map.69 = (f32[32,896]{1,0:T(8,128)}, f32[1,32,4096]{2,1,0:T(8,128)}) custom-call(f32[32,896]{1,0:T(8,128)S(1)} %get-tuple-element.4.p_in, f32[32,4096]{1,0:T(8,128)S(1)} %get-tuple-element.5.q_in), custom_call_target="tpu_custom_call" | custom-call | tf_op jit(solution)/shard_map/pallas_call | solution.py:506

commit v6 on v5

--- a/solution.py
+++ b/solution.py
@@ -18,6 +18,7 @@
 WIDTH = 896
 TOK = 1024
 R = 32
+HR = R // 2
 PARTS = 4
 RH = R // PARTS
 DP = 16
@@ -38,7 +39,7 @@
         key=lambda k: -min(k[0], X - k[0]) - min(k[1], Y - k[1]),
     )
 )
-LAG = 2
+LAG = 3
 
 
 def dot(a, b, dims=NN, precision=None):
@@ -99,10 +100,17 @@
     loads = [
         pltpu.make_async_copy(sk_hbm, sk, load_sem.at[0]),
         pltpu.make_async_copy(g_hbm, g, load_sem.at[1]),
-        pltpu.make_async_copy(gate_hbm, gate, load_sem.at[2]),
-        pltpu.make_async_copy(up_hbm, up, load_sem.at[3]),
-        pltpu.make_async_copy(e_hbm, e, load_sem.at[4]),
     ]
+    for i in range(2):
+        rows = pl.ds(i * TOK // 2, TOK // 2)
+        loads.append(pltpu.make_async_copy(gate_hbm.at[rows], gate.at[rows], load_sem.at[2 + i]))
+        loads.append(pltpu.make_async_copy(up_hbm.at[rows], up.at[rows], load_sem.at[2 + i]))
+    spans = [(0, 512), (512, WIDTH)]
+    error_loads = []
+    for i, (at, to) in enumerate(spans):
+        rows = pl.ds(at, to - at)
+        error_loads.append(pltpu.make_async_copy(e_hbm.at[rows], e.at[rows], load_sem.at[4 + i]))
+    loads += error_loads
     for load in loads:
         load.start()
 
@@ -198,8 +206,7 @@
         )
 
     def errors_copy(j):
-        pair = pl.ds(2 * j, 2)
-        return remote(errors.at[1 - core, pair], errors_in.at[pair], ec_s.at[0], ec_r.at[j], other_core)
+        return remote(errors.at[1 - core, j], errors_in.at[j], ec_s.at[0], ec_r.at[j], other_core)
 
     def chunk(z):
         return jnp.where(z < Y, lax.rem(my + Y - lax.rem(z, Y), Y), Y + lax.rem(mx + X - lax.rem(z, X), X))
@@ -214,15 +221,17 @@
         k = lax.rem(z, 4)
         there = jnp.where(z < 4, mx * Y + lax.rem(my + k, Y), lax.rem(mx + k, X) * Y + my)
         return remote(
-            psum.at[half, z], psum_in.at[half, mz], ps_s.at[0], ps_r.at[0], {"dp": z * 2 + core, "tensor": there}
-        )
-
-    def ra_copy(k):
-        return remote(red, qbuf.at[chunk(mz) * 2 + core], ra_s.at[0], ra_r.at[min(k, Z - k) - 1], z_peer(k))
-
-    def fw_copy(k):
-        held = qbuf.at[chunk(lax.rem(mz + Z - k, Z)) * 2 + core]
-        return remote(held, held, fw_s.at[0], fw_r.at[0], other_core)
+            psum.at[half, z], psum_in.at[half, mz], ps_s.at[0], ps_r.at[half // 2], {"dp": z * 2 + core, "tensor": there}
+        )
+
+    def ra_copy(half, k):
+        return remote(
+            red.at[half], qbuf.at[half, chunk(mz) * 2 + core], ra_s.at[0], ra_r.at[half, min(k, Z - k) - 1], z_peer(k)
+        )
+
+    def fw_copy(half, k):
+        held = qbuf.at[half, chunk(lax.rem(mz + Z - k, Z)) * 2 + core]
+        return remote(held, held, fw_s.at[0], fw_r.at[half], other_core)
 
     def start(copy, order):
         for k in order:
@@ -250,20 +259,19 @@
     pltpu.make_async_copy(*own_a(), gl_r.at[0]).start()
     pltpu.make_async_copy(*own_b(), gl_r.at[1]).start()
 
-    loads[2].wait()
-    loads[3].wait()
-
-    @pl.loop(0, TOK // 64)
-    def _(j):
-        rows = pl.ds(pl.multiple_of(j * 64, 64), 64)
-        v = gate[rows, :].astype(F32)
-        u = up[rows, :].astype(F32)
-        hidden[rows, :WIDTH] = (v / (1.0 + jnp.exp(-v)) * u).astype(BF16)
-        hidden[rows, WIDTH:] = jnp.zeros((64, 4 * LC - WIDTH), BF16)
-
-    loads[4].wait()
-    for at in range(0, WIDTH, 256):
-        to = min(at + 256, WIDTH)
+    for i in range(2):
+        took(gate, load_sem.at[2 + i])
+
+        @pl.loop(i * TOK // 128, (i + 1) * TOK // 128)
+        def _(j):
+            rows = pl.ds(pl.multiple_of(j * 64, 64), 64)
+            v = 0.5 * gate[rows, :].astype(F32)
+            u = up[rows, :].astype(F32)
+            hidden[rows, :WIDTH] = ((v + v * jnp.tanh(v)) * u).astype(BF16)
+            hidden[rows, WIDTH:] = jnp.zeros((64, 4 * LC - WIDTH), BF16)
+
+    for load, (at, to) in zip(error_loads, spans):
+        load.wait()
         leftw[:, at:to] = fold(dot(sks[...], e[at:to, :], NT))
 
     took(proj_in.at[pl.ds(1, TENSOR - 1)], proj_r.at[0])
@@ -323,31 +331,33 @@
 
     whole = split(leftw[:, :WIDTH])
 
-    @pl.loop(0, Z // 2 + LAG)
-    def _(j):
-        @pl.when(j < Z // 2)
+    def turn(n):
+        away = (n + 1) // 2
+        return lax.rem(mz + 4 + jnp.where(lax.rem(n, 2) == 0, away, Z - away), Z)
+
+    @pl.loop(0, Z + LAG)
+    def _(n):
+        @pl.when(n < Z)
         def _():
-            for i, offset in enumerate((4 + j, 3 - j)):
-                place = chunk(lax.rem(mz + offset, Z))
-                for part_of in range(2):
-                    at = pl.multiple_of((2 * place + part_of) * CH, CH)
-                    errors[part_of, 2 * j + i] = fold(dot(whole, e[:, pl.ds(at, CH)]))
-            errors_copy(j).start()
-
-        @pl.when(j >= LAG)
+            place = chunk(turn(n))
+            for part_of in range(2):
+                at = pl.multiple_of((2 * place + part_of) * CH, CH)
+                errors[part_of, n] = fold(dot(whole, e[:, pl.ds(at, CH)]))
+            errors_copy(n).start()
+
+        @pl.when(n >= LAG)
         def _():
-            errors_copy(j - LAG).wait_recv()
-            for i, offset in enumerate((4 + (j - LAG), 3 - (j - LAG))):
-                n = 2 * (j - LAG) + i
-                esum[n] = errors[core, n] + errors_in[n]
-
-                @pl.when(offset == 0)
-                def _():
-                    esum_in[mz] = esum[n]
-
-                @pl.when(offset != 0)
-                def _():
-                    es_copy(n, lax.rem(mz + offset, Z)).start()
+            i = n - LAG
+            errors_copy(i).wait_recv()
+            esum[i] = errors[core, i] + errors_in[i]
+
+            @pl.when(i == Z - 1)
+            def _():
+                esum_in[mz] = esum[i]
+
+            @pl.when(i != Z - 1)
+            def _():
+                es_copy(i, turn(i)).start()
 
     gcols_like = gcols.reshape(2 * TENSOR, OWN, COLS)
     mix_like = mix.reshape(PARTS * 2 * 4, 2 * RH, TOK)
@@ -368,7 +378,7 @@
 
         @pl.when(own_source)
         def _():
-            pltpu.make_async_copy(psum.at[half, mz], psum_in.at[half, mz], ps_r.at[0]).start()
+            pltpu.make_async_copy(psum.at[half, mz], psum_in.at[half, mz], ps_r.at[half // 2]).start()
 
         @pl.when(jnp.logical_not(own_source))
         def _():
@@ -403,25 +413,31 @@
 
     took(esum_in.at[pl.ds(1, Z - 1)], es_r.at[0])
     total = functools.reduce(jnp.add, [esum_in[z] for z in range(Z)])
-    took(psum_in, ps_r.at[0])
-    total = total + jnp.concatenate(
-        [functools.reduce(jnp.add, [psum_in[half, z] for z in range(Z)]) for half in range(PARTS)], axis=0
-    )
-    total = dot(factor, total, NN, HIGH) * (1.0 / (DP * float(WIDTH) ** 0.5))
-    red[...] = total.astype(BF16)
-    start(ra_copy, RING8)
-    qbuf[chunk(mz) * 2 + core] = red[...]
-    fw_copy(0).start()
-
-    for near in range(1, 5):
-        pair = sorted({near, Z - near})
-        took(qbuf.at[pl.ds(0, len(pair))], ra_r.at[near - 1])
-        for k in pair:
-            fw_copy(k).start()
-
-    took(qbuf.at[pl.ds(0, Z)], fw_r.at[0])
-    for p in range(DP):
-        q_ref[:, p * CH : (p + 1) * CH] = qbuf[p].astype(F32)
+
+    sums = []
+    for half in range(2):
+        took(psum_in.at[pl.ds(2 * half, 2)], ps_r.at[half])
+        for part_of in (2 * half, 2 * half + 1):
+            sums.append(
+                total[RH * part_of : RH * (part_of + 1)]
+                + functools.reduce(jnp.add, [psum_in[part_of, z] for z in range(Z)])
+            )
+        to = HR * (half + 1)
+        rows = dot(factor[HR * half : to, :to], jnp.concatenate(sums, axis=0), NN, HIGH)
+        red[half] = (rows * (1.0 / (DP * float(WIDTH) ** 0.5))).astype(BF16)
+        start(functools.partial(ra_copy, half), RING8)
+        qbuf[half, chunk(mz) * 2 + core] = red[half]
+        fw_copy(half, 0).start()
+    for half in range(2):
+        for near in range(1, 5):
+            pair = sorted({near, Z - near})
+            took(qbuf.at[half, pl.ds(0, len(pair))], ra_r.at[half, near - 1])
+            for k in pair:
+                fw_copy(half, k).start()
+    for half in range(2):
+        took(qbuf.at[half, pl.ds(0, Z)], fw_r.at[half])
+        for p in range(DP):
+            q_ref[HR * half : HR * (half + 1), p * CH : (p + 1) * CH] = qbuf[half, p].astype(F32)
 
     psum_like = psum.reshape(PARTS * Z, RH, CH)
 
@@ -433,8 +449,8 @@
     def _():
         took(psum_like, ps_s.at[0])
 
-    took(qbuf.at[pl.ds(0, Z - 1)], ra_s.at[0])
-    took(qbuf.at[pl.ds(0, Z)], fw_s.at[0])
+    took(qbuf.at[0, pl.ds(0, 2 * (Z - 1))], ra_s.at[0])
+    took(qbuf.at[0], fw_s.at[0])
 
 
 def finish(p_in, q_in, p_out, q_out, sem):
@@ -475,9 +491,9 @@
         vmem((PARTS, 2, 4, RH, CH), F32),
         vmem((PARTS, Z, RH, CH), F32),
         vmem((PARTS, Z, RH, CH), F32),
-        vmem((R, CH), BF16),
-        vmem((DP, R, CH), BF16),
-        dma((5,)),
+        vmem((2, HR, CH), BF16),
+        vmem((2, DP, HR, CH), BF16),
+        dma((6,)),
         dma((1,)), dma((1,)),
         dma((1,)), dma((2,)),
         dma((1,)), dma((2,)),
@@ -486,12 +502,12 @@
         dma((1,)), dma((4,)),
         dma((1,)), dma((1,)),
         dma((1,)), dma((PARTS,)),
-        dma((1,)), dma((Z // 2,)),
+        dma((1,)), dma((Z,)),
         dma((1,)), dma((1,)),
         dma((1,)), dma((PARTS,)),
-        dma((1,)), dma((1,)),
-        dma((1,)), dma((4,)),
-        dma((1,)), dma((1,)),
+        dma((1,)), dma((2,)),
+        dma((1,)), dma((2, 4)),
+        dma((1,)), dma((2,)),
     ]
     p_factor, q_factor = pl.pallas_call(
         kernel,

time: 54.9 us -> 54.4 us (level)
  no operation moved by 1% of the time
where the time goes in v6:
time: 54.4 us; the launch traced here: 54.3 us
  Pallas kernels  53.7 us (99%)
  between operations  0.64 us (1%)
    pallas_call x1, Pallas kernels, shards(): pl.pallas_call(kernel, out_shape=(pltpu.VMEM((R, WIDTH), F32), pltpu.VMEM...  52.8 us

profile of v6, /device:TPU:1, one launch (start us, length us, event | category | flops | bytes accessed | tf_op | source)
XLA Modules:
  0.0 54.3 jit_solution(4002075734552271140)
XLA Ops:
  0.6 52.8 %shard_map.68 = (f32[32,896]{1,0:T(8,128)S(1)}, f32[32,4096]{1,0:T(8,128)S(1)}) custom-call(bf16[1024,896]{1,0:T(8,128)(2,1)} %gate_hbm.1, bf16[1024,896]{1,0:T(8,128)(2,1)} %up_hbm.1, bf16[64,4096]{1,0:T(8,128)(2,1)} %g_hbm.1, bf16[896,4096]{1,0:T(8,128)(2,1)} %bitcast.1, f32[32,4096]{1,0:T(8,128)} %sk_hbm.1), custom_call_target="tpu_custom_call" | custom-call | tf_op jit(solution)/shard_map/pallas_call | solution.py:512
  53.5 0.9 %shard_map.69 = (f32[32,896]{1,0:T(8,128)}, f32[1,32,4096]{2,1,0:T(8,128)}) custom-call(f32[32,896]{1,0:T(8,128)S(1)} %get-tuple-element.4.p_in, f32[32,4096]{1,0:T(8,128)S(1)} %get-tuple-element.5.q_in), custom_call_target="tpu_custom_call" | custom-call | tf_op jit(solution)/shard_map/pallas_call | solution.py:522

commit v7 on v6

--- a/solution.py
+++ b/solution.py
@@ -39,7 +39,7 @@
         key=lambda k: -min(k[0], X - k[0]) - min(k[1], Y - k[1]),
     )
 )
-LAG = 3
+LAG = 2
 
 
 def dot(a, b, dims=NN, precision=None):
@@ -251,13 +251,7 @@
 
     pl.semaphore_wait(barrier, TENSOR - 1 + DP - 1 + Z - own_source.astype(jnp.int32))
     start(proj_copy, GRID)
-    start(ga_copy, RING4)
-    start(gb_copy, RING4)
-
-    start(oax_copy, RING4)
-    start(oby_copy, RING4)
-    pltpu.make_async_copy(*own_a(), gl_r.at[0]).start()
-    pltpu.make_async_copy(*own_b(), gl_r.at[1]).start()
+
 
     for i in range(2):
         took(gate, load_sem.at[2 + i])
@@ -274,6 +268,8 @@
         load.wait()
         leftw[:, at:to] = fold(dot(sks[...], e[at:to, :], NT))
 
+    start(ga_copy, RING4)
+    start(gb_copy, RING4)
     took(proj_in.at[pl.ds(1, TENSOR - 1)], proj_r.at[0])
     for j in range(TENSOR // 2):
         a = proj_in[2 * j]
@@ -291,6 +287,10 @@
     for j in range(Z):
         left[core * Z + j] += left_half[j]
     start(ls_copy, RING8)
+    start(oax_copy, RING4)
+    start(oby_copy, RING4)
+    pltpu.make_async_copy(*own_a(), gl_r.at[0]).start()
+    pltpu.make_async_copy(*own_b(), gl_r.at[1]).start()
     took(gcols.at[0, pl.ds(0, 3)], gs_r.at[0])
     for k in range(1, 4):
         start(functools.partial(gax_copy, lax.rem(my + Y - k, Y)), RING4)

time: 54.4 us -> 53.4 us (0.982)
  Pallas kernels: 53.7 us -> 52.7 us
    pallas_call x1, Pallas kernels: 52.8 us -> 51.8 us  [shards(): pl.pallas_call(kernel, out_shape=(pltpu.VMEM((R, WIDTH), F32), pltpu.VMEM...]
where the time goes in v7:
time: 53.4 us; the launch traced here: 53.3 us
  Pallas kernels  52.7 us (99%)
  between operations  0.64 us (1%)
    pallas_call x1, Pallas kernels, shards(): pl.pallas_call(kernel, out_shape=(pltpu.VMEM((R, WIDTH), F32), pltpu.VMEM...  51.8 us

profile of v7, /device:TPU:1, one launch (start us, length us, event | category | flops | bytes accessed | tf_op | source)
XLA Modules:
  0.0 53.3 jit_solution(6918365923925018524)
XLA Ops:
  0.6 51.8 %shard_map.68 = (f32[32,896]{1,0:T(8,128)S(1)}, f32[32,4096]{1,0:T(8,128)S(1)}) custom-call(bf16[1024,896]{1,0:T(8,128)(2,1)} %gate_hbm.1, bf16[1024,896]{1,0:T(8,128)(2,1)} %up_hbm.1, bf16[64,4096]{1,0:T(8,128)(2,1)} %g_hbm.1, bf16[896,4096]{1,0:T(8,128)(2,1)} %bitcast.1, f32[32,4096]{1,0:T(8,128)} %sk_hbm.1), custom_call_target="tpu_custom_call" | custom-call | tf_op jit(solution)/shard_map/pallas_call | solution.py:512
  52.5 0.9 %shard_map.69 = (f32[32,896]{1,0:T(8,128)}, f32[1,32,4096]{2,1,0:T(8,128)}) custom-call(f32[32,896]{1,0:T(8,128)S(1)} %get-tuple-element.4.p_in, f32[32,4096]{1,0:T(8,128)S(1)} %get-tuple-element.5.q_in), custom_call_target="tpu_custom_call" | custom-call | tf_op jit(solution)/shard_map/pallas_call | solution.py:522

commit v8 on v7

--- a/solution.py
+++ b/solution.py
@@ -268,8 +268,9 @@
         load.wait()
         leftw[:, at:to] = fold(dot(sks[...], e[at:to, :], NT))
 
-    start(ga_copy, RING4)
-    start(gb_copy, RING4)
+    for k in RING4:
+        ga_copy(k).start()
+        gb_copy(k).start()
     took(proj_in.at[pl.ds(1, TENSOR - 1)], proj_r.at[0])
     for j in range(TENSOR // 2):
         a = proj_in[2 * j]
@@ -284,11 +285,14 @@
 
     lc_copy().start()
     lc_copy().wait_recv()
-    for j in range(Z):
-        left[core * Z + j] += left_half[j]
-    start(ls_copy, RING8)
-    start(oax_copy, RING4)
-    start(oby_copy, RING4)
+    for k in RING8 + (0,):
+        there = lax.rem(mz + k, Z)
+        left[core * Z + there] += left_half[there]
+        if k:
+            ls_copy(k).start()
+    for k in RING4:
+        oax_copy(k).start()
+        oby_copy(k).start()
     pltpu.make_async_copy(*own_a(), gl_r.at[0]).start()
     pltpu.make_async_copy(*own_b(), gl_r.at[1]).start()
     took(gcols.at[0, pl.ds(0, 3)], gs_r.at[0])
@@ -324,8 +328,9 @@
     mixed = mixed + product_of(1 - core)
     for half in range(PARTS):
         mix[half, 0, 0] = split(mixed[RH * half : RH * (half + 1)])
-        for side in range(2):
-            start(functools.partial(mix_copy, half, side), RING4)
+        for k in RING4:
+            for side in range(2):
+                mix_copy(half, side, k).start()
     for half in range(PARTS):
         mix[half, 1, 0] = mix[half, 0, 0]
 
@@ -370,11 +375,12 @@
                 part[half, part_of, side, (4 - k) % 4] = fold(block[2 * RH * k : 2 * RH * (k + 1)])
 
     def pieces(half):
-        for side in range(2):
-            for k in range(4):
-                psum[half, 4 * side + k] = part[half, core, side, k] + part_in[half, side, k]
-        for offset in RING8:
-            ps_copy(half, lax.rem(mz + offset, Z)).start()
+        for offset in RING8 + (0,):
+            z = lax.rem(mz + offset, Z)
+            side, k = z // 4, lax.rem(z, 4)
+            psum[half, z] = part[half, core, side, k] + part_in[half, side, k]
+            if offset:
+                ps_copy(half, z).start()
 
         @pl.when(own_source)
         def _():

time: 53.4 us -> 53.5 us (level)
  no operation moved by 1% of the time
where the time goes in v8:
time: 53.5 us; the launch traced here: 53.4 us
  Pallas kernels  52.8 us (99%)
  between operations  0.64 us (1%)
    pallas_call x1, Pallas kernels, shards(): pl.pallas_call(kernel, out_shape=(pltpu.VMEM((R, WIDTH), F32), pltpu.VMEM...  51.9 us

profile of v8, /device:TPU:1, one launch (start us, length us, event | category | flops | bytes accessed | tf_op | source)
XLA Modules:
  0.0 53.4 jit_solution(3660516348109528243)
XLA Ops:
  0.6 51.9 %shard_map.68 = (f32[32,896]{1,0:T(8,128)S(1)}, f32[32,4096]{1,0:T(8,128)S(1)}) custom-call(bf16[1024,896]{1,0:T(8,128)(2,1)} %gate_hbm.1, bf16[1024,896]{1,0:T(8,128)(2,1)} %up_hbm.1, bf16[64,4096]{1,0:T(8,128)(2,1)} %g_hbm.1, bf16[896,4096]{1,0:T(8,128)(2,1)} %bitcast.1, f32[32,4096]{1,0:T(8,128)} %sk_hbm.1), custom_call_target="tpu_custom_call" | custom-call | tf_op jit(solution)/shard_map/pallas_call | solution.py:518
  52.5 0.9 %shard_map.69 = (f32[32,896]{1,0:T(8,128)}, f32[1,32,4096]{2,1,0:T(8,128)}) custom-call(f32[32,896]{1,0:T(8,128)S(1)} %get-tuple-element.4.p_in, f32[32,4096]{1,0:T(8,128)S(1)} %get-tuple-element.5.q_in), custom_call_target="tpu_custom_call" | custom-call | tf_op jit(solution)/shard_map/pallas_call | solution.py:528
